TPU v7x, 512 devices: a whole 4x4x16 slice. The times are simulated.
512 devices in a mesh: seq: 16 (over x, z_hi), res: 32 (over y, z_lo, core).
Axes of the slice: x: 4, y: 4, z: 16 (z_hi: 4, z_lo: 4; z = z_hi * 4 + z_lo), core: 2. Of those that a mesh axis runs over, the one named last changes fastest.
Arguments:
- alignment: bfloat16 [32, 2048, 256], P('seq', 'res'), may hold values from -6 to 6
- align_mask: int32 [32, 2048], P('seq', 'res'), may hold values from 0 to 1
- residue_mask: int32 [2048], P('res'), may hold values 0 or 1
- left_weight: bfloat16 [256, 32], replicated, may hold values from -0.375 to 0.375
- right_weight: bfloat16 [256, 32], replicated, may hold values from -0.375 to 0.375
- out_weight: bfloat16 [1024, 128], replicated, may hold values from -0.625 to 0.625
- pair_cotangent: bfloat16 [2048, 32, 64, 128], P('res', None, 'seq'), may hold values from -6 to 6
Outputs:
- pair_update: bfloat16 [2048, 32, 64, 128], P('res', None, 'seq')
- alignment_grad: bfloat16 [32, 2048, 256], P('seq', 'res')
- out_weight_grad: float32 [1024, 128], replicated
All inputs are finite; a program needn't handle non-finite values. No bound on the sum of `residue_mask` on one device may be relied on, other than what follows from the above.
Results may differ from a plain program's by a relative error of at most 0.008.
Values may be sent and summed in bfloat16 or wider, within the bound.
A program may use at most 64 MiB of HBM per device.

v0:
```python
import jax
import jax.numpy as jnp
from jax import lax
from jax.sharding import PartitionSpec as P


def project_rows(alignment, align_mask, residue_mask, left_weight, right_weight):
    values = alignment.astype(jnp.float32)
    center = values - jnp.mean(values, -1, keepdims=True)
    inverse = lax.rsqrt(jnp.mean(center * center, -1, keepdims=True) + 1e-05)
    normal_rows = center * inverse
    rounded = normal_rows.astype(jnp.bfloat16)
    weights = (align_mask * residue_mask[None, :]).astype(jnp.float32)
    left_rows = (
        weights[..., None] * jnp.dot(rounded, left_weight, preferred_element_type=jnp.float32)
    ).astype(jnp.bfloat16)
    right_rows = (
        weights[..., None] * jnp.dot(rounded, right_weight, preferred_element_type=jnp.float32)
    ).astype(jnp.bfloat16)
    return (normal_rows, inverse, weights, left_rows, right_rows)


def norm_backward(normal_rows, inverse, weights, left_grad, right_grad, left_weight, right_weight):
    norm_grad = jnp.dot(
        weights[..., None] * left_grad,
        left_weight.astype(jnp.float32).T,
        precision=lax.Precision.HIGHEST,
    )
    norm_grad = norm_grad + jnp.dot(
        weights[..., None] * right_grad,
        right_weight.astype(jnp.float32).T,
        precision=lax.Precision.HIGHEST,
    )
    first = jnp.mean(norm_grad, -1, keepdims=True)
    second = jnp.mean(norm_grad * normal_rows, -1, keepdims=True)
    return (inverse * (norm_grad - first - normal_rows * second)).astype(jnp.bfloat16)


def shards(
    alignment, align_mask, residue_mask, left_weight, right_weight, out_weight, pair_cotangent
):
    seq_local, res_local = align_mask.shape
    width = left_weight.shape[1]
    res_blocks = pair_cotangent.shape[1]
    offsets = pair_cotangent.shape[2]
    pair_width = pair_cotangent.shape[3]
    normal_rows, inverse, weights, left_rows, right_rows = project_rows(
        alignment, align_mask, residue_mask, left_weight, right_weight
    )
    mask_half = weights.astype(jnp.bfloat16)
    left_flat = left_rows.reshape(seq_local, res_local * width)
    right_flat = right_rows.reshape(seq_local, res_local * width)
    left_all, left_mask = (
        lax.all_gather(left_flat, "seq", axis=0, tiled=True),
        lax.all_gather(mask_half, "seq", axis=0, tiled=True),
    )
    right_part, right_pmask = (
        lax.all_to_all(right_flat, "seq", split_axis=1, concat_axis=0, tiled=True),
        lax.all_to_all(mask_half, "seq", split_axis=1, concat_axis=0, tiled=True),
    )
    right_all, right_mask = (
        lax.all_gather(right_part, "res", axis=1, tiled=True),
        lax.all_gather(right_pmask, "res", axis=1, tiled=True),
    )
    all_seqs = left_all.shape[0]
    columns = res_blocks * offsets
    left_cube = left_all.reshape(all_seqs, res_local, width)
    right_cube = right_all.reshape(all_seqs, columns, width)
    counts = jnp.dot(left_mask.T, right_mask, preferred_element_type=jnp.float32)
    denom = jnp.maximum(counts, 1.0)
    cotangent = pair_cotangent.reshape(res_local, columns, pair_width)
    block = 8

    def step(index, carry):
        pair_out, weight_grad, left_grad, right_grad = carry
        start = index * block
        left_block = lax.dynamic_slice_in_dim(left_cube, start, block, 1)
        outer = jnp.einsum(
            "sic,sjd->ijcd", left_block, right_cube, preferred_element_type=jnp.float32
        )
        outer = outer.reshape(block * columns, width * width).astype(jnp.bfloat16)
        scale_rows = lax.dynamic_slice_in_dim(denom, start, block, 0).reshape(block * columns, 1)
        pair = (jnp.dot(outer, out_weight, preferred_element_type=jnp.float32) / scale_rows).astype(
            jnp.bfloat16
        )
        pair_out = lax.dynamic_update_slice_in_dim(
            pair_out, pair.reshape(block, columns, pair_width), start, 0
        )
        incoming = lax.dynamic_slice_in_dim(cotangent, start, block, 0).reshape(
            block * columns, pair_width
        )
        scaled = (incoming.astype(jnp.float32) / scale_rows).astype(jnp.bfloat16)
        weight_grad = weight_grad + lax.dot_general(
            outer, scaled, (((0,), (0,)), ((), ())), preferred_element_type=jnp.float32
        )
        outer_grad = jnp.dot(scaled, out_weight.T, preferred_element_type=jnp.float32).astype(
            jnp.bfloat16
        )
        outer_grad = outer_grad.reshape(block, columns, width, width)
        left_part = jnp.einsum(
            "ijcd,sjd->sic", outer_grad, right_cube, preferred_element_type=jnp.float32
        )
        left_grad = lax.dynamic_update_slice_in_dim(left_grad, left_part, start, 1)
        right_grad = right_grad + jnp.einsum(
            "ijcd,sic->sjd", outer_grad, left_block, preferred_element_type=jnp.float32
        )
        return (pair_out, weight_grad, left_grad, right_grad)

    start_carry = (
        jnp.zeros((res_local, columns, pair_width), jnp.bfloat16),
        jnp.zeros((width * width, pair_width), jnp.float32),
        jnp.zeros((all_seqs, res_local, width), jnp.float32),
        jnp.zeros((all_seqs, columns, width), jnp.float32),
    )
    pair_out, weight_grad, left_grad, right_grad = lax.fori_loop(
        0, res_local // block, step, start_carry
    )
    weight_total = lax.psum(weight_grad, ("seq", "res"))
    left_own = lax.psum_scatter(
        left_grad.reshape(all_seqs, res_local * width), "seq", scatter_dimension=0, tiled=True
    )
    partial_value = right_grad.reshape(all_seqs, res_blocks, offsets * width)
    moved = lax.all_to_all(partial_value, "seq", split_axis=0, concat_axis=2, tiled=True)
    right_own = lax.psum_scatter(moved, "res", scatter_dimension=1, tiled=True)
    left_own = left_own.reshape(seq_local, res_local, width)
    right_own = right_own.reshape(seq_local, res_local, width)
    alignment_grad = norm_backward(
        normal_rows, inverse, weights, left_own, right_own, left_weight, right_weight
    )
    pair_update = pair_out.reshape(res_local, res_blocks, offsets, pair_width)
    return (pair_update, alignment_grad, weight_total)


def solution(mesh):
    in_specs = (
        P("seq", "res", None),
        P("seq", "res"),
        P("res"),
        P(),
        P(),
        P(),
        P("res", None, "seq", None),
    )
    out_specs = (P("res", None, "seq", None), P("seq", "res", None), P())
    return jax.shard_map(shards, mesh=mesh, in_specs=in_specs, out_specs=out_specs, check_vma=False)
```

profile of v0, /device:TPU:1, one launch (start us, length us, event | category | flops | bytes accessed | tf_op | source)
XLA Modules:
  0.0 1327.8 jit_solution(2413032142410950864)
XLA Ops:
  8.6 18.2 %all-to-all-start.1 = ((bf16[2,16,4]{2,0,1:T(2,128)(2,1)}), bf16[2,16,4]{2,0,1:T(2,128)(2,1)S(1)}, u32[]{:S(2)}, u32[]{:S(2)}) async-start(bf16[2,16,4]{2,0,1:T(2,128)(2,1)} %copy.56), calls=%async_computation.1 | async-start | bytes 16384 | tf_op jit(solution)/shard_map/all_to_all | solution.py:59
  31.2 46.6 %all-gather = bf16[16,2,2048]{2,1,0:T(2,128)(2,1)S(1)} all-gather(bf16[1,2,2048]{2,1,0:T(2,128)(2,1)S(1)} %reshape.115), channel_id=1, replica_groups=mesh['seq'=16,'res'=32] {'seq'}, dimensions={0}, use_global_device_ids=true | all-gather | bytes 139264 | tf_op jit(solution)/shard_map/all_gather | solution.py:54
  77.8 40.8 %all-gather.1 = bf16[16,2,64]{2,1,0:T(2,128)(2,1)S(1)} all-gather(bf16[1,2,64]{2,1,0:T(2,128)(2,1)S(1)} %bitcast.151), channel_id=1, replica_groups=mesh['seq'=16,'res'=32] {'seq'}, dimensions={0}, use_global_device_ids=true | all-gather | bytes 4352 | tf_op jit(solution)/shard_map/all_gather | solution.py:55
  119.7 4.4 all-to-all-start
  124.2 57.6 %all-gather.2 = bf16[32,4,32]{2,1,0:T(4,128)(2,1)S(1)} all-gather(bf16[1,4,32]{2,1,0:T(4,128)(2,1)S(1)} %bitcast.152), channel_id=1, replica_groups=mesh['seq'=16,'res'=32] {'res'}, dimensions={0}, use_global_device_ids=true | all-gather | bytes 8448 | tf_op jit(solution)/shard_map/all_gather | solution.py:63
  182.0 38.9 %all_gather.13 = bf16[32,4096]{1,0:T(8,128)(2,1)S(1)} all-gather(bf16[32,128]{1,0:T(8,128)(2,1)S(1)} %bitcast.149), channel_id=1, replica_groups=mesh['seq'=16,'res'=32] {'res'}, dimensions={1}, use_global_device_ids=true | all-gather | bytes 270336 | tf_op jit(solution)/shard_map/all_gather | solution.py:62
  225.2 122.9 %while.20 = (s32[]{:T(128)}, bf16[64,128,128]{2,1,0:T(8,128)(2,1)}, f32[1024,128]{1,0:T(8,128)S(1)}, f32[32,64,32]{2,1,0:T(8,128)}, f32[32,128,32]{1,0,2:T(8,128...) while((s32[]{:T(128)}, bf16[64,128,128]{2,1,0:T(8,128)(2,1)}, ...), condition=%wide.region_3.0_spmd.clone, body=%wide.region_2.0_spmd.clone.sunk | while | flops 1010302976 | bytes 37351756 | solution.py:115
  232.9 2.6 copy.115
  235.5 2.2 copy.116
  248.3 2.6 copy.115
  250.9 2.2 copy.116
  263.7 2.6 copy.115
  266.2 2.2 copy.116
  279.0 2.6 copy.115
  281.6 2.2 copy.116
  294.4 2.6 copy.115
  309.7 2.6 copy.115
  325.1 2.6 copy.115
  340.5 2.6 copy.115
  350.8 14.1 %all-to-all-start.2 = ((f32[32,32,128]{2,1,0:T(8,128)}), f32[32,32,128]{2,1,0:T(8,128)S(1)}, u32[]{:S(2)}, u32[]{:S(2)}) async-start(f32[32,32,128]{2,1,0:T(8,128)} %reshape.112), calls=%async_computation.2 | async-start | bytes 1048576 | tf_op jit(solution)/shard_map/all_to_all | solution.py:123
  366.3 29.8 %all-to-all-done.2 = f32[32,32,128]{2,1,0:T(8,128)S(1)} async-done(((f32[32,32,128]{2,1,0:T(8,128)}), f32[32,32,128]{2,1,0:T(8,128)S(1)}, u32[]{:S(2)}, u32[]{:S(2)}) %all-to-all-start.2) | async-done | bytes 524320 | tf_op jit(solution)/shard_map/all_to_all | solution.py:123
  401.1 161.6 %all-reduce.8.cloned.1.call-done = f32[32,2048]{1,0:T(8,128)} async-done(((f32[32,2048]{1,0:T(8,128)}), f32[32,2048]{1,0:T(8,128)}) %all-reduce.8.cloned.1.call-update) | async-done | bytes 262160
  564.0 293.4 %all-reduce.10.cloned.1.call-done = f32[2,32,2048]{2,0,1:T(2,128)} async-done(((f32[2,32,2048]{2,0,1:T(2,128)}), f32[2,32,2048]{2,0,1:T(2,128)}) %all-reduce.10.cloned.1.call-update) | async-done | bytes 524304
  860.1 459.3 %all-reduce.6.cloned.1.call-done = f32[1024,128]{1,0:T(8,128)} async-done(((f32[1024,128]{1,0:T(8,128)}), f32[1024,128]{1,0:T(8,128)}) %all-reduce.6.cloned.1.call-update) | async-done | bytes 524304 | tf_op jit(solution)/shard_map/psum | solution.py:118
  (258 shorter events, 117.9 us)
Async XLA Ops:
  7.2 21.6 %copy-start = (bf16[256,32]{0,1:T(8,128)(2,1)S(1)}, bf16[256,32]{0,1:T(8,128)(2,1)}, u32[]{:S(2)}) copy-start(bf16[256,32]{0,1:T(8,128)(2,1)} %param.13) | copy-start | bytes 49156
  8.6 111.1 %all-to-all-start.1 = ((bf16[2,16,4]{2,0,1:T(2,128)(2,1)}), bf16[2,16,4]{2,0,1:T(2,128)(2,1)S(1)}, u32[]{:S(2)}, u32[]{:S(2)}) async-start(bf16[2,16,4]{2,0,1:T(2,128)(2,1)} %copy.56), calls=%async_computation.1 | async-start | bytes 16384 | tf_op jit(solution)/shard_map/all_to_all | solution.py:59
  119.7 62.3 %all-to-all-start = ((bf16[2,16,128]{2,0,1:T(2,128)(2,1)}), bf16[2,16,128]{2,0,1:T(2,128)(2,1)S(1)}, u32[]{:S(2)}, u32[]{:S(2)}) async-start(bf16[2,16,128]{2,0,1:T(2,128)(2,1)} %copy.55), calls=%async_computation | async-start | bytes 16384 | tf_op jit(solution)/shard_map/all_to_all | solution.py:58
  221.7 3.5 copy-start.1
  225.2 3.4 copy-start.3
  229.5 2.5 copy-start.6
  240.6 3.4 copy-start.3
  244.8 2.5 copy-start.6
  255.9 3.4 copy-start.3
  260.2 2.5 copy-start.6
  271.3 3.4 copy-start.3
  286.7 3.4 copy-start.3
  290.9 2.5 copy-start.6
  302.0 3.4 copy-start.3
  317.4 3.4 copy-start.3
  332.8 3.4 copy-start.3
  337.0 2.5 copy-start.6
  349.6 15.5 %copy-start.2 = (f32[32,64,32]{2,1,0:T(8,128)S(1)}, f32[32,64,32]{2,1,0:T(8,128)}, u32[]{:S(2)}) copy-start(f32[32,64,32]{2,1,0:T(8,128)} %get-tuple-element.176) | copy-start | bytes 786436
  350.8 45.3 %all-to-all-start.2 = ((f32[32,32,128]{2,1,0:T(8,128)}), f32[32,32,128]{2,1,0:T(8,128)S(1)}, u32[]{:S(2)}, u32[]{:S(2)}) async-start(f32[32,32,128]{2,1,0:T(8,128)} %reshape.112), calls=%async_computation.2 | async-start | bytes 1048576 | tf_op jit(solution)/shard_map/all_to_all | solution.py:123
  365.0 197.7 %all-reduce.8.cloned.1.call-start = ((), (), s32[]{:S(2)}) async-start(), calls=%async_computation.4 | async-start | bytes 524288
  366.3 491.2 %all-reduce.10.cloned.1.call-start = ((), (), s32[]{:S(2)}) async-start(), calls=%async_computation.5 | async-start | bytes 1048576
  396.1 167.6 %copy-start.9 = (bf16[256,32]{0,1:T(8,128)(2,1)S(1)}, bf16[256,32]{0,1:T(8,128)(2,1)}, u32[]{:S(2)}) copy-start(bf16[256,32]{0,1:T(8,128)(2,1)} %param.12) | copy-start | bytes 49156
  396.4 462.5 %copy-start.5 = (bf16[2,64,256]{2,1,0:T(8,128)(2,1)S(1)}, bf16[2,64,256]{2,1,0:T(8,128)(2,1)}, u32[]{:S(2)}) copy-start(bf16[2,64,256]{2,1,0:T(8,128)(2,1)} %param.9) | copy-start | bytes 196612
  397.8 921.6 %all-reduce.6.cloned.1.call-start = ((), (), s32[]{:S(2)}) async-start(), calls=%async_computation.3 | async-start | bytes 1048576 | tf_op jit(solution)/shard_map/psum | solution.py:118
  (20 other events, 43.1 us)
Sparse Core Ops, SparseCore 0:
  368.7 193.9 all-reduce.7
  566.4 290.9 all-reduce.9
  862.9 456.4 all-reduce.5
where the time goes:
time: 1330 us
  waiting for transfers between devices  944 us (71%)
  blocking collectives  184 us (14%)
  local copies, waits for them, and re-layouts  75.7 us (6%)
  matrix products  43.1 us (3%)
  starting transfers between devices  36.8 us (3%)
  other arithmetic  28.2 us (2%)
  between operations  14.6 us (1%)
    psum x1, waiting for transfers between devices, shards(): weight_total = lax.psum(weight_grad, ('seq', 'res'))  459 us
    unnamed x5, waiting for transfers between devices  455 us
    all_gather x1, blocking collectives, shards(): lax.all_gather(right_pmask, 'res', axis=1, tiled=True)  57.6 us
    all_gather x1, blocking collectives, shards(): lax.all_gather(left_flat, 'seq', axis=0, tiled=True)  46.6 us
    all_gather x1, blocking collectives, shards(): lax.all_gather(mask_half, 'seq', axis=0, tiled=True)  40.8 us
    all_gather x1, blocking collectives, shards(): lax.all_gather(right_part, 'res', axis=1, tiled=True)  38.9 us
    all_to_all x1, waiting for transfers between devices, shards(): lax.all_to_all(partial_value, 'seq', split_axis=0, concat_axis=2, tiled=T...  29.8 us
  transfers between devices with their start and end apart: 6, of which 4 were waited for; matrix products, arithmetic and copies ran while one was open for 1% of the time, Pallas kernels for 0%

commit v1 on v0

v1 whole, which is shorter than its diff:
```python
import jax
import jax.numpy as jnp
from jax import lax
from jax.experimental import pallas as pl
from jax.experimental.pallas import tpu as pltpu
from jax.sharding import PartitionSpec as P

F32 = jnp.float32
BF16 = jnp.bfloat16
MESH = pl.DeviceIdType.MESH

NX, NZ, NYZ = 4, 4, 16
NSEQ = NX * NZ
SEQS, RES, WIDTH, CH, PAIR = 32, 64, 32, 256, 128
COLS = 128
BLOCK = 8
NT_DIMS = (((1,), (1,)), ((), ()))


def iota(shape, dim):
    return lax.broadcasted_iota(jnp.int32, shape, dim)


def onehot(condition, kind=BF16):
    return jnp.where(condition, 1.0, 0.0).astype(kind)


def mm(a, b):
    return jnp.dot(a, b, preferred_element_type=F32)


def mm_nt(a, b):
    return lax.dot_general(a, b, NT_DIMS, preferred_element_type=F32)


def place():
    a = lax.axis_index("seq")
    b = lax.axis_index("res")
    x, zh = a // NZ, a % NZ
    core, yz = b % 2, b // 2
    return a, b, x, zh, core, yz


def partners_barrier(a, b, x, zh, core, yz):
    sem = pltpu.get_barrier_semaphore()

    def signal(seq, res):
        pl.semaphore_signal(sem, inc=1, device_id=(seq, res), device_id_type=MESH)

    for k in range(1, NZ):
        signal(x * NZ + (zh + k) % NZ, b)
    for k in range(1, NX):
        signal(((x + k) % NX) * NZ + zh, b)
    signal(a, yz * 2 + (1 - core))

    @pl.loop(1, NYZ)
    def _(k):
        signal(a, ((yz + k) % NYZ) * 2 + core)

    pl.semaphore_wait(sem, (NZ - 1) + (NX - 1) + 1 + (NYZ - 1))


def remote(src, dst, send, recv, seq, res):
    return pltpu.make_async_remote_copy(
        src_ref=src, dst_ref=dst, send_sem=send, recv_sem=recv, device_id=(seq, res), device_id_type=MESH
    )


def normalise(al_ref):
    values = al_ref[...].astype(F32)
    center = values - jnp.mean(values, -1, keepdims=True)
    inverse = lax.rsqrt(jnp.mean(center * center, -1, keepdims=True) + 1e-05)
    return center * inverse, inverse


def weight_rows(am_ref, rm_ref):
    return (am_ref[...] * rm_ref[...]).astype(F32)


def as_column(row):
    n = row.shape[1]
    return jnp.sum(jnp.where(iota((n, n), 0) == iota((n, n), 1), row, 0.0), axis=1, keepdims=True)


def gather_kernel(
    al_ref, am_ref, rm_ref, wl_ref, wr_ref, g_ref, x_ref, mask_ref,
    z_send, z_recv, x_send, x_recv, r_send, r_recv, c_send, c_recv,
):
    a, b, x, zh, core, yz = place()
    partners_barrier(a, b, x, zh, core, yz)
    normal, _ = normalise(al_ref)
    rounded = normal.astype(BF16)
    w2 = weight_rows(am_ref, rm_ref)
    total = jnp.zeros((RES, 128), F32)
    for s in range(2):
        lane, row = iota((WIDTH, 128), 1), iota((WIDTH, 128), 0)
        left_at = onehot(lane == row + s * WIDTH)
        right_at = onehot(lane == row + 2 * WIDTH + s * WIDTH)
        both = (mm(wl_ref[...], left_at) + mm(wr_ref[...], right_at)).astype(BF16)
        total = total + as_column(w2[s : s + 1]) * mm(rounded[s * RES : (s + 1) * RES], both)
    mask_ref[...] = jnp.zeros((16, 128), F32)
    mask_ref[0:2, 0:RES] = w2
    g_ref[a, 0:RES] = total.astype(BF16)
    g_ref[a, RES : RES + 16] = mask_ref[...].astype(BF16)

    def z_copy(k):
        other = (zh + k) % NZ
        return remote(g_ref.at[a], g_ref.at[a], z_send.at[k], z_recv.at[zh], x * NZ + other, b)

    for k in range(1, NZ):
        z_copy(k).start()
    for k in range(1, NZ):
        other = (zh + k) % NZ
        slot = g_ref.at[x * NZ + other]
        remote(slot, slot, z_send.at[k], z_recv.at[other], a, b).wait_recv()

    def x_copy(k):
        slab = g_ref.at[pl.ds(x * NZ, NZ)]
        return remote(slab, slab, x_send.at[k], x_recv.at[x], ((x + k) % NX) * NZ + zh, b)

    for k in range(1, NX):
        x_copy(k).start()
    for k in range(1, NX):
        other = (x + k) % NX
        slab = g_ref.at[pl.ds(other * NZ, NZ)]
        remote(slab, slab, x_send.at[k], x_recv.at[other], a, b).wait_recv()

    blocks = g_ref[:, 0:RES, :].reshape(NSEQ * RES, 128)
    r, col = iota((64, NSEQ * RES), 0), iota((64, NSEQ * RES), 1)
    target = (2 * ((r % 32) // 4) + r // 32) * RES + 4 * a + r % 4
    picked = mm(onehot(col == target), blocks)
    even = pltpu.roll(picked[0:32], 64, 1)
    chunk = jnp.where(iota((32, 128), 1) < 64, even, picked[32:64])
    masks = g_ref[:, RES : RES + 16, :].astype(F32)[:, 0:8, :].reshape(128, 128).astype(BF16)
    r, lane = iota((16, 128), 0), iota((16, 128), 1)
    chunk_mask = mm_nt(onehot((lane == 4 * a + r) & (r < 4)), masks)
    x_ref[core, yz, 0:32] = chunk.astype(BF16)
    x_ref[core, yz, 32:48] = chunk_mask.astype(BF16)

    def r_copy(k):
        other = (yz + k) % NYZ
        slot = x_ref.at[core, yz]
        return remote(slot, slot, r_send.at[k], r_recv.at[yz], a, other * 2 + core)

    @pl.loop(1, NYZ)
    def _(k):
        r_copy(k).start()

    @pl.loop(1, NYZ)
    def _(k):
        other = (yz + k) % NYZ
        slot = x_ref.at[core, other]
        remote(slot, slot, r_send.at[k], r_recv.at[other], a, b).wait_recv()

    c_copy = remote(x_ref.at[core], x_ref.at[core], c_send, c_recv, a, yz * 2 + (1 - core))
    c_copy.start()
    for k in range(1, NZ):
        z_copy(k).wait_send()
    for k in range(1, NX):
        x_copy(k).wait_send()

    @pl.loop(1, NYZ)
    def _(k):
        r_copy(k).wait_send()

    c_copy.wait_send()
    slab = x_ref.at[1 - core]
    remote(slab, slab, c_send, c_recv, a, b).wait_recv()


def pair_kernel(
    g_ref, x_ref, w_ref, ct_ref, pair_ref, lm_ref, rd_ref,
    wf, wn, w4, lf, l2, lt, rf, rmf, perm, rds, rt, rden, nc, tb, sc, rg, lgs, dw,
):
    step = pl.program_id(0)

    @pl.when(step == 0)
    def _():
        wf[...] = w_ref[...].astype(F32)
        for d in range(WIDTH):
            piece = wf[pl.ds(d, WIDTH, stride=WIDTH), :].astype(BF16)
            wn[:, d * PAIR : (d + 1) * PAIR] = piece
            for q in range(4):
                w4[q * WIDTH : (q + 1) * WIDTH, d * PAIR : (d + 1) * PAIR] = piece
        blocks = g_ref[:, 0:RES, :].reshape(NSEQ * RES, 128)
        row, lane = iota((128, 128), 0), iota((128, 128), 1)
        for s in range(2):
            moved = mm(blocks, onehot((row == lane + s * WIDTH) & (lane < WIDTH)))
            for n in range(NSEQ):
                lf[pl.ds(2 * n + s, RES, stride=SEQS), :] = moved[n * RES : (n + 1) * RES]
        l2[...] = lf[...].astype(BF16)
        eye = onehot(iota((WIDTH, 128), 0) == iota((WIDTH, 128), 1))
        for n in range(RES // BLOCK):
            rows = BLOCK * SEQS
            lt[n] = mm_nt(eye, l2[n * rows : (n + 1) * rows, :]).astype(BF16)
        for core in range(2):
            for yz in range(NYZ):
                part = x_ref[core, yz].astype(F32)
                at = (yz * 2 + core) * 4
                for t in range(8):
                    rf[at : at + 4, t * 128 : (t + 1) * 128] = part[4 * t : 4 * t + 4]
                rmf[at : at + 4, :] = part[32:36]
        size = WIDTH * SEQS
        for n in range(8):
            r, col = iota((size // 8, size), 0) + n * (size // 8), iota((size // 8, size), 1)
            perm[n * (size // 8) : (n + 1) * (size // 8), :] = onehot(col == (r % 32) * 32 + r // 32)
        right = rf[...].astype(BF16)
        rds[...] = mm(right, perm[...]).astype(BF16)
        rt[...] = mm_nt(perm[...], right).astype(BF16)
        masks = g_ref[:, RES : RES + 16, :].astype(F32)[:, 0:8, :].reshape(128, 128).astype(BF16)
        counts = mm(rmf[...].astype(BF16), masks)
        rden[...] = 1.0 / jnp.maximum(counts, 1.0)
        rg[...] = jnp.zeros_like(rg)
        dw[...] = jnp.zeros_like(dw)

    rows = BLOCK * SEQS
    l2c = l2[pl.ds(pl.multiple_of(step * rows, rows), rows), 0:WIDTH]
    scale = pltpu.roll(rden[...], lax.rem(128 - step * BLOCK, 128), 1)
    for d2 in range(WIDTH // 2):
        part = mm(l2c, wn[:, d2 * 256 : (d2 + 1) * 256]).astype(BF16)
        for h in range(2):
            d = 2 * d2 + h
            for k in range(BLOCK):
                nc[d * SEQS : (d + 1) * SEQS, k * PAIR : (k + 1) * PAIR] = part[
                    k * SEQS : (k + 1) * SEQS, h * PAIR : (h + 1) * PAIR
                ]
    for k in range(BLOCK):
        sc[:, k * PAIR : (k + 1) * PAIR] = (ct_ref[k].astype(F32) * scale[:, k : k + 1]).astype(BF16)
    for k2 in range(BLOCK // 2):
        part = mm(rds[...], nc[:, k2 * 256 : (k2 + 1) * 256])
        for h in range(2):
            k = 2 * k2 + h
            pair_ref[k] = (part[:, h * PAIR : (h + 1) * PAIR] * scale[:, k : k + 1]).astype(BF16)
    rg[...] += mm_nt(sc[...], nc[...])
    for k2 in range(BLOCK // 2):
        part = mm(rt[...], sc[:, k2 * 256 : (k2 + 1) * 256]).astype(BF16)
        for h in range(2):
            k = 2 * k2 + h
            for d in range(WIDTH):
                tb[k * SEQS : (k + 1) * SEQS, d * PAIR : (d + 1) * PAIR] = part[
                    d * SEQS : (d + 1) * SEQS, h * PAIR : (h + 1) * PAIR
                ]
    lgs[pl.ds(pl.multiple_of(step * rows, rows), rows), :] = mm_nt(tb[...], w4[...])
    dw[...] += mm(lt[step], tb[...])

    @pl.when(step == pl.num_programs(0) - 1)
    def _():
        rf[...] = mm(rg[...].astype(BF16), perm[...])
        for core in range(2):
            for yz in range(NYZ):
                d = yz * 2 + core
                lf[0:32, :] = jnp.concatenate(
                    [rf[4 * d : 4 * d + 4, t * 128 : (t + 1) * 128] for t in range(8)], axis=0
                )
                rd_ref[core, yz, 0:32] = lf[0:32, :].astype(BF16)
                rd_ref[core, yz, 32:64] = dw[:, d * PAIR : (d + 1) * PAIR].astype(BF16)
        lane = iota((32, 128), 1) // WIDTH
        for n in range(NSEQ):
            out = lgs[pl.ds(2 * n, 32, stride=SEQS), :]
            for q in range(1, 4):
                piece = lgs[pl.ds((q // 2) * 32 * SEQS + 2 * n + q % 2, 32, stride=SEQS), :]
                out = jnp.where(lane == q, piece, out)
            lm_ref[n] = out.astype(BF16)


def reduce_kernel(
    rd_ref, lm_ref, al_ref, am_ref, rm_ref, wl_ref, wr_ref, ag_ref, dw_ref,
    core_in, half, half_in, seq_all, left_x, left_half, left_z, fin,
    c_send, c_recv, lx_send, lx_recv, r_send, r_recv, lz_send, lz_recv,
    z_send, z_recv, x_send, x_recv, f_send, f_recv, e_send, e_recv,
):
    a, b, x, zh, core, yz = place()
    partners_barrier(a, b, x, zh, core, yz)
    c_copy = remote(rd_ref.at[1 - core], core_in, c_send, c_recv, a, yz * 2 + (1 - core))
    c_copy.start()

    def lx_copy(k):
        other = (x + k) % NX
        return remote(
            lm_ref.at[pl.ds(other * NZ, NZ)], left_x.at[x], lx_send.at[k], lx_recv.at[x], other * NZ + zh, b
        )

    for k in range(1, NX):
        lx_copy(k).start()
    c_copy.wait_recv()
    for n in range(NYZ):
        half[n] = (rd_ref[core, n].astype(F32) + core_in[n].astype(F32)).astype(BF16)

    def r_copy(k):
        other = (yz + k) % NYZ
        return remote(half.at[other], half_in.at[yz], r_send.at[k], r_recv.at[yz], a, other * 2 + core)

    @pl.loop(1, NYZ)
    def _(k):
        r_copy(k).start()

    half_in[yz] = half[yz]
    left_x[x] = lm_ref[pl.ds(x * NZ, NZ)]
    for k in range(1, NX):
        other = (x + k) % NX
        slab = left_x.at[other]
        remote(slab, slab, lx_send.at[k], lx_recv.at[other], a, b).wait_recv()
    left = left_x[0].astype(F32)
    for n in range(1, NX):
        left = left + left_x[n].astype(F32)
    left_half[...] = left.astype(BF16)

    def lz_copy(k):
        other = (zh + k) % NZ
        return remote(left_half.at[other], left_z.at[zh], lz_send.at[k], lz_recv.at[zh], x * NZ + other, b)

    for k in range(1, NZ):
        lz_copy(k).start()
    left_z[zh] = left_half[zh]

    @pl.loop(1, NYZ)
    def _(k):
        other = (yz + k) % NYZ
        slot = half_in.at[other]
        remote(slot, slot, r_send.at[k], r_recv.at[other], a, b).wait_recv()

    chunk = half_in[0].astype(F32)
    for n in range(1, NYZ):
        chunk = chunk + half_in[n].astype(F32)
    seq_all[a] = chunk.astype(BF16)

    def z_copy(k):
        other = (zh + k) % NZ
        return remote(seq_all.at[a], seq_all.at[a], z_send.at[k], z_recv.at[zh], x * NZ + other, b)

    for k in range(1, NZ):
        z_copy(k).start()
    for k in range(1, NZ):
        other = (zh + k) % NZ
        slot = seq_all.at[x * NZ + other]
        remote(slot, slot, z_send.at[k], z_recv.at[other], a, b).wait_recv()

    def x_copy(k):
        slab = seq_all.at[pl.ds(x * NZ, NZ)]
        return remote(slab, slab, x_send.at[k], x_recv.at[x], ((x + k) % NX) * NZ + zh, b)

    for k in range(1, NX):
        x_copy(k).start()
    for k in range(1, NZ):
        other = (zh + k) % NZ
        slot = left_z.at[other]
        remote(slot, slot, lz_send.at[k], lz_recv.at[other], a, b).wait_recv()
    left = left_z[0].astype(F32)
    for n in range(1, NZ):
        left = left + left_z[n].astype(F32)
    normal, inverse = normalise(al_ref)
    w2 = weight_rows(am_ref, rm_ref)
    for k in range(1, NX):
        other = (x + k) % NX
        slab = seq_all.at[pl.ds(other * NZ, NZ)]
        remote(slab, slab, x_send.at[k], x_recv.at[other], a, b).wait_recv()

    block = seq_all[0, 32:64].astype(F32)
    for n in range(1, NSEQ):
        block = block + seq_all[n, 32:64].astype(F32)
    fin[core, yz] = block.astype(BF16)

    def f_copy(k):
        other = (yz + k) % NYZ
        slot = fin.at[core, yz]
        return remote(slot, slot, f_send.at[k], f_recv.at[yz], a, other * 2 + core)

    @pl.loop(1, NYZ)
    def _(k):
        f_copy(k).start()

    rows = seq_all[:, 0:32, :].reshape(NSEQ * 32, 128)
    r, col = iota((RES, NSEQ * 32), 0), iota((RES, NSEQ * 32), 1)
    right = mm(onehot(col == (r // 4) * 32 + (a // 2) * 4 + r % 4), rows).astype(BF16)
    left_high = left.astype(BF16)
    left_low = (left - left_high.astype(F32)).astype(BF16)
    row, lane = iota((128, WIDTH), 0), iota((128, WIDTH), 1)
    for s in range(2):
        right_at = mm_nt(onehot(row == lane + (a % 2) * 64 + s * WIDTH), wr_ref[...]).astype(BF16)
        parts = []
        for h in range(2):
            left_at = mm_nt(onehot(row == lane + (2 * h + s) * WIDTH), wl_ref[...]).astype(BF16)
            parts.append(mm(left_high, left_at) + mm(left_low, left_at))
        grad = (jnp.concatenate(parts, axis=0) + mm(right, right_at)) * as_column(w2[s : s + 1])
        span = slice(s * RES, (s + 1) * RES)
        first = jnp.mean(grad, -1, keepdims=True)
        second = jnp.mean(grad * normal[span], -1, keepdims=True)
        ag_ref[span] = (inverse[span] * (grad - first - normal[span] * second)).astype(BF16)

    @pl.loop(1, NYZ)
    def _(k):
        other = (yz + k) % NYZ
        slot = fin.at[core, other]
        remote(slot, slot, f_send.at[k], f_recv.at[other], a, b).wait_recv()

    e_copy = remote(fin.at[core], fin.at[core], e_send, e_recv, a, yz * 2 + (1 - core))
    e_copy.start()
    c_copy.wait_send()
    for k in range(1, NX):
        lx_copy(k).wait_send()
        x_copy(k).wait_send()
    for k in range(1, NZ):
        lz_copy(k).wait_send()
        z_copy(k).wait_send()

    @pl.loop(1, NYZ)
    def _(k):
        r_copy(k).wait_send()
        f_copy(k).wait_send()

    e_copy.wait_send()
    slab = fin.at[1 - core]
    remote(slab, slab, e_send, e_recv, a, b).wait_recv()
    for c in range(2):
        for n in range(NYZ):
            dw_ref[pl.ds(n * 2 + c, WIDTH, stride=WIDTH), :] = fin[c, n].astype(F32)


def vmem():
    return pl.BlockSpec(memory_space=pltpu.VMEM)


def whole(shape):
    return pl.BlockSpec(shape, lambda i: (0,) * len(shape))


def dma(n):
    return pltpu.SemaphoreType.DMA((n,))


def shards(alignment, align_mask, residue_mask, left_weight, right_weight, out_weight, pair_cotangent):
    al = alignment.reshape(2 * RES, CH)
    rm = residue_mask.reshape(1, RES)
    one = pltpu.SemaphoreType.DMA
    gathered, rights = pl.pallas_call(
        gather_kernel,
        out_shape=(
            jax.ShapeDtypeStruct((NSEQ, RES + 16, 128), BF16),
            jax.ShapeDtypeStruct((2, NYZ, 48, 128), BF16),
        ),
        in_specs=[vmem()] * 5,
        out_specs=(vmem(), vmem()),
        scratch_shapes=[
            pltpu.VMEM((16, 128), F32),
            dma(NZ), dma(NZ), dma(NX), dma(NX), dma(NYZ), dma(NYZ), one, one,
        ],
        compiler_params=pltpu.CompilerParams(
            collective_id=0, has_side_effects=True, vmem_limit_bytes=24 * 1024 * 1024
        ),
        name="gather_rows",
    )(al, align_mask, rm, left_weight, right_weight)

    steps = RES // BLOCK
    size = WIDTH * SEQS
    tile = pl.BlockSpec((BLOCK, COLS, PAIR), lambda i: (i, 0, 0))
    pair, left_msg, rd = pl.pallas_call(
        pair_kernel,
        grid=(steps,),
        out_shape=(
            jax.ShapeDtypeStruct((RES, COLS, PAIR), BF16),
            jax.ShapeDtypeStruct((NSEQ, 32, 128), BF16),
            jax.ShapeDtypeStruct((2, NYZ, 64, 128), BF16),
        ),
        in_specs=[whole(gathered.shape), whole(rights.shape), whole((size, PAIR)), tile],
        out_specs=(tile, whole((NSEQ, 32, 128)), whole((2, NYZ, 64, 128))),
        scratch_shapes=[
            pltpu.VMEM((size, PAIR), F32),
            pltpu.VMEM((WIDTH, WIDTH * PAIR), BF16),
            pltpu.VMEM((128, WIDTH * PAIR), BF16),
            pltpu.VMEM((RES * SEQS, 128), F32),
            pltpu.VMEM((RES * SEQS, 128), BF16),
            pltpu.VMEM((steps, WIDTH, BLOCK * SEQS), BF16),
            pltpu.VMEM((COLS, size), F32),
            pltpu.VMEM((COLS, 128), F32),
            pltpu.VMEM((size, size), BF16),
            pltpu.VMEM((COLS, size), BF16),
            pltpu.VMEM((size, COLS), BF16),
            pltpu.VMEM((COLS, 128), F32),
            pltpu.VMEM((size, BLOCK * PAIR), BF16),
            pltpu.VMEM((BLOCK * SEQS, WIDTH * PAIR), BF16),
            pltpu.VMEM((COLS, BLOCK * PAIR), BF16),
            pltpu.VMEM((COLS, size), F32),
            pltpu.VMEM((RES * SEQS, 128), F32),
            pltpu.VMEM((WIDTH, WIDTH * PAIR), F32),
        ],
        compiler_params=pltpu.CompilerParams(vmem_limit_bytes=48 * 1024 * 1024),
        name="pair_update",
    )(gathered, rights, out_weight, pair_cotangent.reshape(RES, COLS, PAIR))

    ag, dw = pl.pallas_call(
        reduce_kernel,
        out_shape=(
            jax.ShapeDtypeStruct((2 * RES, CH), BF16),
            jax.ShapeDtypeStruct((size, PAIR), F32),
        ),
        in_specs=[vmem()] * 7,
        out_specs=(vmem(), vmem()),
        scratch_shapes=[
            pltpu.VMEM((NYZ, 64, 128), BF16),
            pltpu.VMEM((NYZ, 64, 128), BF16),
            pltpu.VMEM((NYZ, 64, 128), BF16),
            pltpu.VMEM((NSEQ, 64, 128), BF16),
            pltpu.VMEM((NX, NZ, 32, 128), BF16),
            pltpu.VMEM((NZ, 32, 128), BF16),
            pltpu.VMEM((NZ, 32, 128), BF16),
            pltpu.VMEM((2, NYZ, 32, 128), BF16),
            one, one, dma(NX), dma(NX), dma(NYZ), dma(NYZ), dma(NZ), dma(NZ),
            dma(NZ), dma(NZ), dma(NX), dma(NX), dma(NYZ), dma(NYZ), one, one,
        ],
        compiler_params=pltpu.CompilerParams(
            collective_id=1, has_side_effects=True, vmem_limit_bytes=24 * 1024 * 1024
        ),
        name="reduce_gradients",
    )(rd, left_msg, al, align_mask, rm, left_weight, right_weight)
    return (
        pair.reshape(pair_cotangent.shape),
        ag.reshape(alignment.shape),
        dw,
    )


def solution(mesh):
    in_specs = (
        P("seq", "res", None),
        P("seq", "res"),
        P("res"),
        P(),
        P(),
        P(),
        P("res", None, "seq", None),
    )
    out_specs = (P("res", None, "seq", None), P("seq", "res", None), P())
    return jax.shard_map(shards, mesh=mesh, in_specs=in_specs, out_specs=out_specs, check_vma=False)
```

time: 1330 us -> 114 us (0.09)
  waiting for transfers between devices: 944 us -> 0 us
  blocking collectives: 184 us -> 0 us
  Pallas kernels: 0 us -> 105 us
  local copies, waits for them, and re-layouts: 75.7 us -> 7.85 us
  matrix products: 43.1 us -> 0 us
  starting transfers between devices: 36.8 us -> 0 us
  other arithmetic: 28.2 us -> 0 us
  between operations: 14.6 us -> 0.7 us
    psum x1 -> x0, waiting for transfers between devices: 459 us -> none  [shards(): weight_total = lax.psum(weight_grad, ('seq', 'res'))]
    unnamed x5 -> x0, waiting for transfers between devices: 455 us -> none
    all_gather x4 -> x0, blocking collectives: 184 us -> none  [the longest x1 57.6 us: shards(): lax.all_gather(right_pmask, 'res', axis=1, tiled=True)]
    pallas_call x0 -> x3, Pallas kernels: none -> 105 us  [the longest x1 37.2 us: shards(): pl.pallas_call(reduce_kernel, out_shape=(jax.ShapeDtypeStruct((2 * RES, C...]
    dot_general x53 -> x0, matrix products: 43.1 us -> none  [the longest x8 10.6 us: step(): jnp.einsum('ijcd,sic->sjd', outer_grad, left_block, preferred_element_typ...]
    all_to_all x3 -> x0, starting transfers between devices: 36.7 us -> none  [the longest x1 18.2 us: shards(): lax.all_to_all(mask_half, 'seq', split_axis=1, concat_axis=0, tiled=True)]
    convert_element_type x18 -> x0, local copies, waits for them, and re-layouts: 31.5 us -> none  [the longest x8 20.5 us: step(): jnp.dot(scaled, out_weight.T, preferred_element_type=jnp.float32)]
    all_to_all x3 -> x0, waiting for transfers between devices: 29.8 us -> none  [the longest x1 29.8 us: shards(): lax.all_to_all(partial_value, 'seq', split_axis=0, concat_axis=2, tiled=T...]
  transfers between devices with their start and end apart: 6 -> 0, of which waited for: 4 -> 0; matrix products, arithmetic and copies ran while one was open for 1% -> 0% of each run, Pallas kernels for 0% -> 0%
where the time goes in v1:
time: 114 us
  Pallas kernels  105 us (92%)
  local copies, waits for them, and re-layouts  7.85 us (7%)
    pallas_call x1, Pallas kernels, shards(): pl.pallas_call(reduce_kernel, out_shape=(jax.ShapeDtypeStruct((2 * RES, C...  37.2 us
    pallas_call x1, Pallas kernels, shards(): pl.pallas_call(gather_kernel, out_shape=(jax.ShapeDtypeStruct((NSEQ, RES...  36.8 us
    pallas_call x1, Pallas kernels, shards(): pl.pallas_call(pair_kernel, grid=(steps,), out_shape=(jax.ShapeDtypeStruc...  31.2 us
    unnamed x20, local copies, waits for them, and re-layouts  7.85 us

profile of v1, /device:TPU:1, one launch (start us, length us, event | category | flops | bytes accessed | tf_op | source)
XLA Modules:
  0.0 113.7 jit_solution(5537121491238760589)
XLA Ops:
  0.6 0.0 copy-start.5
  0.6 0.0 copy-start.7
  0.7 0.0 copy-start.3
  0.7 0.9 copy.10.wl_ref
  1.5 0.8 copy.11.wr_ref
  2.4 0.0 copy-start.2
  2.4 0.8 copy-done.2
  3.2 0.0 copy-start.4
  3.2 0.7 copy-done.4
  3.9 0.0 copy-start.6
  3.9 0.7 copy-done.6
  4.6 36.8 %gather_rows.1 = (bf16[16,80,128]{2,1,0:T(8,128)(2,1)S(1)}, bf16[2,16,48,128]{3,2,1,0:T(8,128)(2,1)S(1)}) custom-call(bf16[128,256]{1,0:T(8,128)(2,1)S(1)} %bitcast.6, s32[2,64]{1,0:T(2,128)S(1)} %copy-done.4, s32[1,64]{1,0:T(1,128)S(1)} %bitcast.9, bf16[256,32]{1,0:T(8,128)(2,1)S(1)} %copy.10.wl_ref, bf16[256,32]{1,0:T(8,128)(2,1)S(1)} %copy.11.wr_ref), custom_call_target="tpu_custom_call" | custom-call | tf_op jit(solution)/shard_map/gather_rows/pallas_call | solution.py:435
  41.4 0.0 copy-start
  41.4 1.6 %copy-done = bf16[64,32,4,128]{3,2,1,0:T(4,128)(2,1)S(1)} copy-done((bf16[64,32,4,128]{3,2,1,0:T(4,128)(2,1)S(1)}, bf16[64,32,4,128]{3,2,1,0:T(4,128)(2,1)}, u32[]{:S(2)}) %copy-start) | copy-done | bytes 2097176
  43.0 0.0 copy-start.1
  43.0 0.9 copy-done.1
  43.9 31.2 %pair_update.1 = (bf16[64,128,128]{2,1,0:T(8,128)(2,1)}, bf16[16,32,128]{2,1,0:T(8,128)(2,1)S(1)}, bf16[2,16,64,128]{3,2,1,0:T(8,128)(2,1)S(1)}) custom-call(bf16[16,80,128]{2,1,0:T(8,128)(2,1)S(1)} %get-tuple-element.10.g_ref, bf16[2,16,48,128]{3,2,1,0:T(8,128)(2,1)S(1)} %get-tuple-element.11.x_ref, bf16[1024,128]{1,0:T(8,128)(2,1)S(1)} %copy-done.1, ...), custom_call_target="tpu_custom_call" | custom-call | tf_op jit(solution)/shard_map/pair_update/pallas_call | solution.py:456
  75.1 0.0 copy-done.5
  75.1 0.0 copy-done.7
  75.1 0.0 copy-done.3
  75.1 37.2 %reduce_gradients.1 = (bf16[128,256]{1,0:T(8,128)(2,1)S(1)}, f32[1024,128]{1,0:T(8,128)S(1)}) custom-call(bf16[2,16,64,128]{3,2,1,0:T(8,128)(2,1)S(1)} %get-tuple-element.13.rd_ref, bf16[16,32,128]{2,1,0:T(8,128)(2,1)S(1)} %get-tuple-element.14.lm_ref, bf16[128,256]{1,0:T(8,128)(2,1)S(1)} %bitcast.7, s32[2,64]{1,0:T(2,128)S(1)} %copy-done.5, ...), custom_call_target="tpu_custom_call" | custom-call | tf_op jit(solution)/shard_map/reduce_gradients/pallas_call | solution.py:490
  112.3 0.6 copy.16
  112.9 0.8 copy.17
Async XLA Ops:
  0.6 74.5 %copy-start.5 = (s32[2,64]{1,0:T(2,128)S(1)}, s32[2,64]{1,0:T(2,128)}, u32[]{:S(2)}) copy-start(s32[2,64]{1,0:T(2,128)} %am_ref.3) | copy-start | bytes 1540
  0.6 74.5 %copy-start.7 = (s32[64]{0:T(128)S(1)}, s32[64]{0:T(128)}, u32[]{:S(2)}) copy-start(s32[64]{0:T(128)} %param.9) | copy-start | bytes 772
  0.7 74.4 %copy-start.3 = (bf16[2,64,256]{2,1,0:T(8,128)(2,1)S(1)}, bf16[2,64,256]{2,1,0:T(8,128)(2,1)}, u32[]{:S(2)}) copy-start(bf16[2,64,256]{2,1,0:T(8,128)(2,1)} %param.7) | copy-start | bytes 196612
  2.4 0.8 copy-start.2
  3.2 0.7 copy-start.4
  3.9 0.7 copy-start.6
  41.4 1.6 %copy-start = (bf16[64,32,4,128]{3,2,1,0:T(4,128)(2,1)S(1)}, bf16[64,32,4,128]{3,2,1,0:T(4,128)(2,1)}, u32[]{:S(2)}) copy-start(bf16[64,32,4,128]{3,2,1,0:T(4,128)(2,1)} %param.13) | copy-start | bytes 6291460
  43.0 0.9 copy-start.1

commit v2 on v0

v2 whole, which is shorter than its diff:
```python
import jax
import jax.numpy as jnp
from jax import lax
from jax.experimental import pallas as pl
from jax.experimental.pallas import tpu as pltpu
from jax.sharding import PartitionSpec as P

F32 = jnp.float32
BF16 = jnp.bfloat16
MESH = pl.DeviceIdType.MESH

NSEQ, SEQS, RES, WIDTH, CH, PAIR, COLS = 16, 32, 64, 32, 256, 128, 128
BLOCK = 8
STEPS = RES // BLOCK
SIZE = WIDTH * SEQS
NT_DIMS = (((1,), (1,)), ((), ()))


def iota(shape, dim):
    return lax.broadcasted_iota(jnp.int32, shape, dim)


def onehot(condition):
    return jnp.where(condition, 1.0, 0.0).astype(BF16)


def mm(a, b):
    return jnp.dot(a, b, preferred_element_type=F32)


def mm_nt(a, b):
    return lax.dot_general(a, b, NT_DIMS, preferred_element_type=F32)


def split(value):
    high = value.astype(BF16)
    return high, (value - high.astype(F32)).astype(BF16)


def as_column(row):
    n = row.shape[1]
    return jnp.sum(jnp.where(iota((n, n), 0) == iota((n, n), 1), row, 0.0), axis=1, keepdims=True)


def remote(src, dst, send, recv, device):
    return pltpu.make_async_remote_copy(
        src_ref=src, dst_ref=dst, send_sem=send, recv_sem=recv, device_id=device, device_id_type=MESH
    )


class Group:
    def __init__(self, count, me, device_of, source_of, slot_of, send, recv):
        self.count, self.me, self.device_of = count, me, device_of
        self.source_of, self.slot_of, self.send, self.recv = source_of, slot_of, send, recv

    def each(self, body):
        if self.count <= 4:
            for k in range(1, self.count):
                body(k, (self.me + k) % self.count)
        else:

            @pl.loop(1, self.count)
            def _(k):
                body(k, (self.me + k) % self.count)

    def out(self, k, other):
        return remote(
            self.source_of(other), self.slot_of(self.me), self.send.at[k], self.recv.at[self.me],
            self.device_of(other),
        )

    def start(self):
        self.each(lambda k, other: self.out(k, other).start())

    def wait(self):
        def body(k, other):
            slot = self.slot_of(other)
            remote(slot, slot, self.send.at[k], self.recv.at[other], self.device_of(other)).wait_recv()

        self.each(body)

    def sent(self):
        self.each(lambda k, other: self.out(k, other).wait_send())


def total(ref, first, count, span=slice(None)):
    value = ref[first, span].astype(F32)
    for n in range(1, count):
        value = value + ref[first + n, span].astype(F32)
    return value


def kernel(
    al_hbm, am_hbm, rm_hbm, wl_hbm, wr_hbm, w_hbm, ct_hbm,
    pair_ref, ag_ref, dw_ref,
    al_ref, am_ref, rm_ref, wl_ref, wr_ref, w_ref, ct_ref, in_sem,
    mask_ref, rsend, ra, rb, xr, lall,
    wf, wn, w4, lf, l2, lt, perm, rp, rm_all, rds, rt, rden, n_all, t_all, sc, rg, lgs, dw,
    wmsg, wcin, whalf, wxin, wz, fin,
    rmsg, rcin, rhalf, rxin, rzs, rzin,
    lmsg, lx, lhalf, lz,
    c_send, c_recv,
    z_r_send, z_r_recv, z_l_send, z_l_recv, xy_r_send, xy_r_recv, x_l_send, x_l_recv,
    xy_w_send, xy_w_recv, z_w_send, z_w_recv, xy_f_send, xy_f_recv,
    xy_g_send, xy_g_recv, z_g_send, z_g_recv, x_g_send, x_g_recv, zl_g_send, zl_g_recv,
):
    a = lax.axis_index("seq")
    b = lax.axis_index("res")
    x, zh, core, y, zl = a // 4, a % 4, b % 2, b // 8, (b // 2) % 4
    xy, z = x * 4 + y, zh * 4 + zl
    z_device = lambda o: (x * 4 + o // 4, (y * 4 + o % 4) * 2 + core)
    xy_device = lambda o: ((o // 4) * 4 + zh, ((o % 4) * 4 + zl) * 2 + core)
    zh_device = lambda o: (x * 4 + o, b)
    x_device = lambda o: (o * 4 + zh, b)
    other_core = (a, b + 1 - 2 * core)

    def core_copy(n, src, dst):
        return remote(src, dst, c_send.at[n], c_recv.at[n], other_core)

    loads = [
        pltpu.make_async_copy(src, dst, in_sem.at[n])
        for n, (src, dst) in enumerate(
            (
                (al_hbm, al_ref), (am_hbm, am_ref), (rm_hbm, rm_ref), (wl_hbm, wl_ref), (wr_hbm, wr_ref),
                (w_hbm, w_ref), (ct_hbm, ct_ref),
            )
        )
    ]
    for load in loads:
        load.start()
    barrier = pltpu.get_barrier_semaphore()

    @pl.loop(1, 16)
    def _(k):
        pl.semaphore_signal(barrier, inc=1, device_id=z_device((z + k) % 16), device_id_type=MESH)
        pl.semaphore_signal(barrier, inc=1, device_id=xy_device((xy + k) % 16), device_id_type=MESH)

    pl.semaphore_signal(barrier, inc=1, device_id=other_core, device_id_type=MESH)
    for load in loads[:5]:
        load.wait()

    values = al_ref[...].astype(F32)
    center = values - jnp.mean(values, -1, keepdims=True)
    inverse = lax.rsqrt(jnp.mean(center * center, -1, keepdims=True) + 1e-05)
    rounded = (center * inverse).astype(BF16)
    w2 = (am_ref[...] * rm_ref[...]).astype(F32)
    row, lane = iota((128, WIDTH), 0), iota((128, WIDTH), 1)
    lanes = iota((RES, 128), 1)
    right = jnp.zeros((RES, 128), F32)
    left = jnp.zeros((32, 128), F32)
    for s in range(2):
        column = as_column(w2[s : s + 1])
        mine = rounded[s * RES : (s + 1) * RES]
        right_at = mm(onehot(row == lane + s * WIDTH), wr_ref[...]).astype(BF16)
        right = right + column * (mm_nt(mine, right_at) + jnp.where(lanes == 2 * WIDTH + s, 1.0, 0.0))
        for h in range(2):
            left_at = mm(onehot(row == lane + (2 * h + s) * WIDTH), wl_ref[...]).astype(BF16)
            span = slice(h * 32, (h + 1) * 32)
            left = left + column[span] * mm_nt(mine[span], left_at)
    r, col = iota((RES, RES), 0), iota((RES, RES), 1)
    order = onehot(col == ((r // 4) % 4) * 16 + (r // 16) * 4 + r % 4)
    right = mm(order, right.astype(BF16)).astype(BF16)
    for n in range(4):
        rsend[n] = right[n * 16 : (n + 1) * 16]
    mask_ref[...] = jnp.zeros((16, 128), F32)
    mask_ref[0:2, 0:RES] = w2
    lall[a, 0:32] = left.astype(BF16)
    lall[a, 32:48] = mask_ref[...].astype(BF16)

    loads[5].wait()
    wf[...] = w_ref[...].astype(F32)
    for d in range(WIDTH):
        piece = wf[pl.ds(d, WIDTH, stride=WIDTH), :].astype(BF16)
        wn[:, d * PAIR : (d + 1) * PAIR] = piece
        for q in range(4):
            w4[q * WIDTH : (q + 1) * WIDTH, d * PAIR : (d + 1) * PAIR] = piece

    pl.semaphore_wait(barrier, 31)

    z_r = Group(16, z, z_device, lambda o: rsend.at[o // 4], lambda n: ra.at[n], z_r_send, z_r_recv)
    z_l = Group(
        4, zh, zh_device, lambda o: lall.at[a], lambda n: lall.at[x * 4 + n], z_l_send, z_l_recv
    )
    z_r.start()
    z_l.start()
    ra[z] = rsend[zh]
    for n in range(8):
        r, col = iota((SIZE // 8, SIZE), 0) + n * (SIZE // 8), iota((SIZE // 8, SIZE), 1)
        perm[n * (SIZE // 8) : (n + 1) * (SIZE // 8), :] = onehot(col == (r % 32) * 32 + r // 32)
    z_r.wait()

    r, col = iota((256, 256), 0), iota((256, 256), 1)
    order = onehot(col == ((r // 16) % 4) * 64 + ((r // 4) % 4) * 16 + (r // 64) * 4 + r % 4)
    moved = mm(order, ra[...].reshape(256, 128))
    lanes = iota((16, 128), 1)
    for n in range(4):
        part = [moved[n * 64 + h * 16 : n * 64 + (h + 1) * 16] for h in range(4)]
        masks = jnp.zeros((16, 128), F32)
        for h in range(4):
            own = jnp.where((lanes >= 64) & (lanes < 66), part[h], 0.0)
            masks = masks + pltpu.roll(own, (x * 8 + h * 2 + 64) % 128, 1)
        for t in range(2):
            tile = jnp.where(lanes < 64, part[2 * t], pltpu.roll(part[2 * t + 1], 64, 1))
            rb[n, t * 16 : (t + 1) * 16] = tile.astype(BF16)
        rb[n, 32:48] = masks.astype(BF16)
    xy_r = Group(16, xy, xy_device, lambda o: rb.at[o // 4], lambda n: xr.at[core, n], xy_r_send, xy_r_recv)
    x_l = Group(
        4, x, x_device, lambda o: lall.at[pl.ds(x * 4, 4)], lambda n: lall.at[pl.ds(n * 4, 4)],
        x_l_send, x_l_recv,
    )
    xy_r.start()
    xr[core, xy] = rb[x]
    z_l.wait()
    x_l.start()
    loads[6].wait()
    xy_r.wait()

    c_r = core_copy(0, xr.at[core], xr.at[core])
    c_r.start()
    x_l.wait()
    blocks = lall[:, 0:32, :].reshape(NSEQ * 32, 128)
    row, lane = iota((128, 128), 0), iota((128, 128), 1)
    for h in range(2):
        for s in range(2):
            moved = mm(blocks, onehot((row == lane + (2 * h + s) * WIDTH) & (lane < WIDTH)))
            for n in range(NSEQ):
                lf[pl.ds(h * 32 * SEQS + 2 * n + s, 32, stride=SEQS), :] = moved[n * 32 : (n + 1) * 32]
    l2[...] = lf[...].astype(BF16)
    eye = onehot(iota((WIDTH, 128), 0) == iota((WIDTH, 128), 1))
    rows = BLOCK * SEQS
    for n in range(STEPS):
        lt[n] = mm_nt(eye, l2[n * rows : (n + 1) * rows, :]).astype(BF16)
    masks = lall[:, 32:48, :].astype(F32)[:, 0:8, :].reshape(128, 128).astype(BF16)
    r, col = iota((128, 128), 0), iota((128, 128), 1)
    left_mask = mm(onehot((r < SEQS) & (col == (r // 2) * 8 + r % 2)), masks).astype(BF16)
    slab = xr.at[1 - core]
    core_copy(0, slab, slab).wait_recv()

    for c in range(2):
        for n in range(4):
            at = slice((c * 4 + n) * 16, (c * 4 + n + 1) * 16)
            rm_all[at] = sum(xr[c, m * 4 + n, 32:48].astype(F32) for m in range(4))
            for m in range(4):
                for t in range(2):
                    rp[at, m * 256 + t * 128 : m * 256 + (t + 1) * 128] = xr[
                        c, m * 4 + n, t * 16 : (t + 1) * 16
                    ]
    r, col = iota((128, 128), 0), iota((128, 128), 1)
    order = onehot(col == ((r // 4) % 2) * 64 + (r // 32) * 16 + ((r // 8) % 4) * 4 + r % 4)
    right_mask = mm(order, rm_all[...].astype(BF16)).astype(BF16)
    rden[...] = 1.0 / jnp.maximum(mm(right_mask, left_mask), 1.0)
    right = mm(order, rp[...]).astype(BF16)
    rds[...] = mm(right, perm[...]).astype(BF16)
    rt[...] = mm_nt(perm[...], right).astype(BF16)

    def scale_of(step):
        return pltpu.roll(rden[...], lax.rem(128 - step * BLOCK, 128), 1)

    dw[...] = jnp.zeros_like(dw)

    @pl.loop(0, STEPS)
    def _(step):
        scale = scale_of(step)
        for k in range(BLOCK):
            sc[step, :, k * PAIR : (k + 1) * PAIR] = (
                ct_ref[step * BLOCK + k].astype(F32) * scale[:, k : k + 1]
            ).astype(BF16)
        for k2 in range(BLOCK // 2):
            part = mm(rt[...], sc[step, :, k2 * 256 : (k2 + 1) * 256]).astype(BF16)
            for h in range(2):
                k = 2 * k2 + h
                for d in range(WIDTH):
                    t_all[step, k * SEQS : (k + 1) * SEQS, d * PAIR : (d + 1) * PAIR] = part[
                        d * SEQS : (d + 1) * SEQS, h * PAIR : (h + 1) * PAIR
                    ]
        dw[...] += mm(lt[step], t_all[step])

    for c in range(2):
        for n in range(16):
            d = c * 16 + n
            wmsg[c, n] = dw[:, d * PAIR : (d + 1) * PAIR].astype(BF16)
    c_w = core_copy(1, wmsg.at[1 - core], wcin)
    c_w.start()

    rg[...] = jnp.zeros_like(rg)

    def right_part(step):
        rows = BLOCK * SEQS
        l2c = l2[pl.ds(pl.multiple_of(step * rows, rows), rows), 0:WIDTH]
        for d2 in range(WIDTH // 2):
            part = mm(l2c, wn[:, d2 * 256 : (d2 + 1) * 256]).astype(BF16)
            for h in range(2):
                d = 2 * d2 + h
                for k in range(BLOCK):
                    n_all[step, d * SEQS : (d + 1) * SEQS, k * PAIR : (k + 1) * PAIR] = part[
                        k * SEQS : (k + 1) * SEQS, h * PAIR : (h + 1) * PAIR
                    ]
        rg[...] += mm_nt(sc[step], n_all[step])

    pl.loop(0, 3)(right_part)

    core_copy(1, wcin, wcin).wait_recv()
    for n in range(16):
        whalf[n] = (wmsg[core, n].astype(F32) + wcin[n].astype(F32)).astype(BF16)
    xy_w = Group(16, xy, xy_device, lambda o: whalf.at[o], lambda n: wxin.at[n], xy_w_send, xy_w_recv)
    xy_w.start()
    wxin[xy] = whalf[xy]

    pl.loop(3, STEPS)(right_part)
    grads = mm(rg[...].astype(BF16), perm[...]).astype(BF16)
    r, col = iota((128, 128), 0), iota((128, 128), 1)
    order = onehot(col == ((r // 16) % 4) * 32 + ((r // 4) % 4) * 8 + (r // 64) * 4 + r % 4)
    grads = mm(order, grads).astype(BF16)
    for c in range(2):
        for m in range(4):
            for n in range(4):
                at = slice((c * 4 + n) * 16, (c * 4 + n + 1) * 16)
                for t in range(2):
                    rmsg[c, m * 4 + n, t * 16 : (t + 1) * 16] = grads[
                        at, m * 256 + t * 128 : m * 256 + (t + 1) * 128
                    ]
    c_g = core_copy(2, rmsg.at[1 - core], rcin)
    c_g.start()

    xy_w.wait()
    wz[z] = total(wxin, 0, 16).astype(BF16)
    z_w = Group(16, z, z_device, lambda o: wz.at[z], lambda n: wz.at[n], z_w_send, z_w_recv)
    z_w.start()

    def left_part(step):
        rows = BLOCK * SEQS
        lgs[pl.ds(pl.multiple_of(step * rows, rows), rows), :] = mm_nt(t_all[step], w4[...])

    pl.loop(0, 4)(left_part)
    core_copy(2, rcin, rcin).wait_recv()
    for n in range(16):
        rhalf[n] = (rmsg[core, n].astype(F32) + rcin[n].astype(F32)).astype(BF16)
    xy_g = Group(16, xy, xy_device, lambda o: rhalf.at[o], lambda n: rxin.at[n], xy_g_send, xy_g_recv)
    xy_g.start()
    rxin[xy] = rhalf[xy]
    pl.loop(4, STEPS)(left_part)
    lane = iota((32, 128), 1) // WIDTH
    for n in range(NSEQ):
        out = lgs[pl.ds(2 * n, 32, stride=SEQS), :]
        for q in range(1, 4):
            piece = lgs[pl.ds((q // 2) * 32 * SEQS + 2 * n + q % 2, 32, stride=SEQS), :]
            out = jnp.where(lane == q, piece, out)
        lmsg[n] = out.astype(BF16)
    x_g = Group(
        4, x, x_device, lambda o: lmsg.at[pl.ds(o * 4, 4)], lambda n: lx.at[n], x_g_send, x_g_recv
    )
    x_g.start()
    lx[x] = lmsg[pl.ds(x * 4, 4)]

    def pair_part(step):
        scale = scale_of(step)
        for k2 in range(BLOCK // 2):
            part = mm(rds[...], n_all[step, :, k2 * 256 : (k2 + 1) * 256])
            for h in range(2):
                k = 2 * k2 + h
                pair_ref[step * BLOCK + k] = (
                    part[:, h * PAIR : (h + 1) * PAIR] * scale[:, k : k + 1]
                ).astype(BF16)

    pl.loop(0, 4)(pair_part)

    xy_g.wait()
    sums = [total(rxin, m * 4, 4).astype(BF16) for m in range(4)]
    r, col = iota((64, 64), 0), iota((64, 64), 1)
    order = onehot(col == ((r // 4) % 4) * 16 + (r // 16) * 4 + r % 4)
    for t in range(2):
        moved = mm(order, jnp.concatenate([v[t * 16 : (t + 1) * 16] for v in sums], axis=0))
        for h in range(2):
            own = moved if h == 0 else pltpu.roll(moved, 64, 1)
            for n in range(4):
                rzs[(2 * t + h) * 4 + n] = own[n * 16 : (n + 1) * 16].astype(BF16)
    z_g = Group(16, z, z_device, lambda o: rzs.at[o], lambda n: rzin.at[n], z_g_send, z_g_recv)
    z_g.start()
    rzin[z] = rzs[z]

    x_g.wait()
    lhalf[...] = total(lx, 0, 4).astype(BF16)
    zl_g = Group(4, zh, zh_device, lambda o: lhalf.at[o], lambda n: lz.at[n], zl_g_send, zl_g_recv)
    zl_g.start()
    lz[zh] = lhalf[zh]

    z_w.wait()
    fin[core, xy] = total(wz, 0, 16).astype(BF16)
    xy_f = Group(
        16, xy, xy_device, lambda o: fin.at[core, xy], lambda n: fin.at[core, n], xy_f_send, xy_f_recv
    )
    xy_f.start()
    pl.loop(4, STEPS)(pair_part)

    values = al_ref[...].astype(F32)
    center = values - jnp.mean(values, -1, keepdims=True)
    inverse = lax.rsqrt(jnp.mean(center * center, -1, keepdims=True) + 1e-05)
    normal = center * inverse
    w2 = (am_ref[...] * rm_ref[...]).astype(F32)
    zl_g.wait()
    left = split(total(lz, 0, 4))
    z_g.wait()
    r, col = iota((RES, RES), 0), iota((RES, RES), 1)
    order = onehot(col == ((r // 4) % 4) * 16 + (r // 16) * 4 + r % 4)
    right = split(jnp.concatenate([total(rzin, n * 4, 4) for n in range(4)], axis=0))
    right = [mm(order, v).astype(BF16) for v in right]
    row, lane = iota((128, WIDTH), 0), iota((128, WIDTH), 1)
    for s in range(2):
        right_at = mm(onehot(row == lane + s * WIDTH), wr_ref[...]).astype(BF16)
        parts = []
        for h in range(2):
            left_at = mm(onehot(row == lane + (2 * h + s) * WIDTH), wl_ref[...]).astype(BF16)
            parts.append(mm(left[0], left_at) + mm(left[1], left_at))
        grad = jnp.concatenate(parts, axis=0) + mm(right[0], right_at) + mm(right[1], right_at)
        grad = grad * as_column(w2[s : s + 1])
        span = slice(s * RES, (s + 1) * RES)
        first = jnp.mean(grad, -1, keepdims=True)
        second = jnp.mean(grad * normal[span], -1, keepdims=True)
        ag_ref[span] = (inverse[span] * (grad - first - normal[span] * second)).astype(BF16)

    xy_f.wait()
    c_f = core_copy(3, fin.at[core], fin.at[core])
    c_f.start()
    for group in (z_r, z_l, xy_r, x_l, xy_w, z_w, xy_f, xy_g, z_g, x_g, zl_g):
        group.sent()
    for copy in (c_r, c_w, c_g, c_f):
        copy.wait_send()
    slab = fin.at[1 - core]
    core_copy(3, slab, slab).wait_recv()
    for c in range(2):
        for n in range(16):
            dw_ref[pl.ds(c * 16 + n, WIDTH, stride=WIDTH), :] = fin[c, n].astype(F32)


def shards(alignment, align_mask, residue_mask, left_weight, right_weight, out_weight, pair_cotangent):
    dma = pltpu.SemaphoreType.DMA
    vmem = pltpu.VMEM
    pair, ag, dw = pl.pallas_call(
        kernel,
        out_shape=(
            jax.ShapeDtypeStruct((RES, COLS, PAIR), BF16),
            jax.ShapeDtypeStruct((2 * RES, CH), BF16),
            jax.ShapeDtypeStruct((SIZE, PAIR), F32),
        ),
        in_specs=[pl.BlockSpec(memory_space=pl.ANY)] * 7,
        out_specs=(pl.BlockSpec(memory_space=pltpu.VMEM),) * 3,
        scratch_shapes=[
            vmem((2 * RES, CH), BF16), vmem((2, RES), jnp.int32), vmem((1, RES), jnp.int32),
            vmem((WIDTH, CH), BF16), vmem((WIDTH, CH), BF16), vmem((SIZE, PAIR), BF16),
            vmem((RES, COLS, PAIR), BF16), dma((7,)),
            vmem((16, 128), F32), vmem((4, 16, 128), BF16), vmem((16, 16, 128), BF16),
            vmem((4, 48, 128), BF16), vmem((2, 16, 48, 128), BF16), vmem((NSEQ, 48, 128), BF16),
            vmem((SIZE, PAIR), F32), vmem((WIDTH, WIDTH * PAIR), BF16), vmem((128, WIDTH * PAIR), BF16),
            vmem((RES * SEQS, 128), F32), vmem((RES * SEQS, 128), BF16),
            vmem((STEPS, WIDTH, BLOCK * SEQS), BF16), vmem((SIZE, SIZE), BF16),
            vmem((COLS, SIZE), BF16), vmem((COLS, 128), F32), vmem((COLS, SIZE), BF16),
            vmem((SIZE, COLS), BF16), vmem((COLS, 128), F32),
            vmem((STEPS, SIZE, BLOCK * PAIR), BF16), vmem((STEPS, BLOCK * SEQS, WIDTH * PAIR), BF16),
            vmem((STEPS, COLS, BLOCK * PAIR), BF16), vmem((COLS, SIZE), F32),
            vmem((RES * SEQS, 128), F32), vmem((WIDTH, WIDTH * PAIR), F32),
            vmem((2, 16, 32, 128), BF16), vmem((16, 32, 128), BF16), vmem((16, 32, 128), BF16),
            vmem((16, 32, 128), BF16), vmem((16, 32, 128), BF16), vmem((2, 16, 32, 128), BF16),
            vmem((2, 16, 32, 128), BF16), vmem((16, 32, 128), BF16), vmem((16, 32, 128), BF16),
            vmem((16, 32, 128), BF16), vmem((16, 16, 128), BF16), vmem((16, 16, 128), BF16),
            vmem((NSEQ, 32, 128), BF16), vmem((4, 4, 32, 128), BF16), vmem((4, 32, 128), BF16),
            vmem((4, 32, 128), BF16),
            dma((4,)), dma((4,)),
            dma((16,)), dma((16,)), dma((4,)), dma((4,)), dma((16,)), dma((16,)), dma((4,)), dma((4,)),
            dma((16,)), dma((16,)), dma((16,)), dma((16,)), dma((16,)), dma((16,)),
            dma((16,)), dma((16,)), dma((16,)), dma((16,)), dma((4,)), dma((4,)), dma((4,)), dma((4,)),
        ],
        compiler_params=pltpu.CompilerParams(
            collective_id=0, has_side_effects=True, vmem_limit_bytes=58 * 1024 * 1024
        ),
        name="pair_update",
    )(
        alignment.reshape(2 * RES, CH), align_mask, residue_mask.reshape(1, RES), left_weight.T, right_weight.T,
        out_weight, pair_cotangent.reshape(RES, COLS, PAIR),
    )
    return pair.reshape(pair_cotangent.shape), ag.reshape(alignment.shape), dw


def solution(mesh):
    in_specs = (
        P("seq", "res", None),
        P("seq", "res"),
        P("res"),
        P(),
        P(),
        P(),
        P("res", None, "seq", None),
    )
    out_specs = (P("res", None, "seq", None), P("seq", "res", None), P())
    return jax.shard_map(shards, mesh=mesh, in_specs=in_specs, out_specs=out_specs, check_vma=False)
```

time: 1330 us -> 90.9 us (0.07)
  waiting for transfers between devices: 944 us -> 0 us
  blocking collectives: 184 us -> 0 us
  Pallas kernels: 0 us -> 84.1 us
  local copies, waits for them, and re-layouts: 75.7 us -> 5.96 us
  matrix products: 43.1 us -> 0 us
  starting transfers between devices: 36.8 us -> 0 us
  other arithmetic: 28.2 us -> 0 us
  between operations: 14.6 us -> 0.66 us
    psum x1 -> x0, waiting for transfers between devices: 459 us -> none  [shards(): weight_total = lax.psum(weight_grad, ('seq', 'res'))]
    unnamed x5 -> x0, waiting for transfers between devices: 455 us -> none
    all_gather x4 -> x0, blocking collectives: 184 us -> none  [the longest x1 57.6 us: shards(): lax.all_gather(right_pmask, 'res', axis=1, tiled=True)]
    pallas_call x0 -> x1, Pallas kernels: none -> 84.1 us  [shards(): pl.pallas_call(kernel, out_shape=(jax.ShapeDtypeStruct((RES, COLS, PAIR),...]
    dot_general x53 -> x0, matrix products: 43.1 us -> none  [the longest x8 10.6 us: step(): jnp.einsum('ijcd,sic->sjd', outer_grad, left_block, preferred_element_typ...]
    all_to_all x3 -> x0, starting transfers between devices: 36.7 us -> none  [the longest x1 18.2 us: shards(): lax.all_to_all(mask_half, 'seq', split_axis=1, concat_axis=0, tiled=True)]
    convert_element_type x18 -> x0, local copies, waits for them, and re-layouts: 31.5 us -> none  [the longest x8 20.5 us: step(): jnp.dot(scaled, out_weight.T, preferred_element_type=jnp.float32)]
    all_to_all x3 -> x0, waiting for transfers between devices: 29.8 us -> none  [the longest x1 29.8 us: shards(): lax.all_to_all(partial_value, 'seq', split_axis=0, concat_axis=2, tiled=T...]
  transfers between devices with their start and end apart: 6 -> 0, of which waited for: 4 -> 0; matrix products, arithmetic and copies ran while one was open for 1% -> 0% of each run, Pallas kernels for 0% -> 0%
where the time goes in v2:
time: 90.9 us; the launch traced here: 90.7 us
  Pallas kernels  84.1 us (93%)
  local copies, waits for them, and re-layouts  5.96 us (7%)
    pallas_call x1, Pallas kernels, shards(): pl.pallas_call(kernel, out_shape=(jax.ShapeDtypeStruct((RES, COLS, PAIR),...  84.1 us
    unnamed x7, local copies, waits for them, and re-layouts  5.96 us

profile of v2, /device:TPU:1, one launch (start us, length us, event | category | flops | bytes accessed | tf_op | source)
XLA Modules:
  0.0 90.7 jit_solution(3776441874674199054)
XLA Ops:
  0.6 84.1 %pair_update.1 = (bf16[64,128,128]{2,1,0:T(8,128)(2,1)}, bf16[128,256]{1,0:T(8,128)(2,1)}, f32[1024,128]{1,0:T(8,128)}) custom-call(bf16[128,256]{1,0:T(8,128)(2,1)} %bitcast.9, s32[2,64]{1,0:T(2,128)} %am_hbm.1, s32[1,64]{1,0:T(1,128)} %bitcast.13, bf16[32,256]{1,0:T(8,128)(2,1)} %bitcast.11, bf16[32,256]{1,0:T(8,128)(2,1)} %bitcast.12, ...), custom_call_target="tpu_custom_call" | custom-call | tf_op jit(solution)/shard_map/pair_update/pallas_call | solution.py:438
  84.7 0.0 copy-start.1
  84.7 0.0 copy-start
  84.7 4.5 %copy.13 = bf16[64,32,4,128]{3,2,1,0:T(4,128)(2,1)} copy(bf16[64,32,4,128]{3,2,1,0:T(4,128)(2,1)} %bitcast.8) | data formatting | bytes 4194304
  89.3 0.0 copy-done.1
  89.3 0.6 copy.14
  89.9 0.0 copy-done
  89.9 0.8 copy.15
Async XLA Ops:
  84.7 4.6 %copy-start.1 = (bf16[128,256]{1,0:T(8,128)(2,1)S(1)}, bf16[128,256]{1,0:T(8,128)(2,1)}, u32[]{:S(2)}) copy-start(bf16[128,256]{1,0:T(8,128)(2,1)} %get-tuple-element.7) | copy-start | bytes 196612
  84.7 5.2 %copy-start = (f32[1024,128]{1,0:T(8,128)S(1)}, f32[1024,128]{1,0:T(8,128)}, u32[]{:S(2)}) copy-start(f32[1024,128]{1,0:T(8,128)} %get-tuple-element.14) | copy-start | bytes 1572868

commit v3 on v2

--- a/solution.py
+++ b/solution.py
@@ -49,19 +49,20 @@
 
 
 class Group:
-    def __init__(self, count, me, device_of, source_of, slot_of, send, recv):
+    def __init__(self, count, me, device_of, source_of, slot_of, send, recv, peer_of=None):
         self.count, self.me, self.device_of = count, me, device_of
+        self.peer_of = peer_of or (lambda k: (me + k) % count)
         self.source_of, self.slot_of, self.send, self.recv = source_of, slot_of, send, recv
 
     def each(self, body):
         if self.count <= 4:
-            for k in range(1, self.count):
-                body(k, (self.me + k) % self.count)
+            for k in (2, 1, 3) if self.count == 4 else (1,):
+                body(k, self.peer_of(k))
         else:
 
-            @pl.loop(1, self.count)
+            @pl.loop(0, self.count - 1)
             def _(k):
-                body(k, (self.me + k) % self.count)
+                body(k, self.peer_of(k))
 
     def out(self, k, other):
         return remote(
@@ -92,11 +93,11 @@
 
 def kernel(
     al_hbm, am_hbm, rm_hbm, wl_hbm, wr_hbm, w_hbm, ct_hbm,
-    pair_ref, ag_ref, dw_ref,
+    pair_ref, ag_ref, fin,
     al_ref, am_ref, rm_ref, wl_ref, wr_ref, w_ref, ct_ref, in_sem,
     mask_ref, rsend, ra, rb, xr, lall,
     wf, wn, w4, lf, l2, lt, perm, rp, rm_all, rds, rt, rden, n_all, t_all, sc, rg, lgs, dw,
-    wmsg, wcin, whalf, wxin, wz, fin,
+    wmsg, wcin, whalf, wxin, wz,
     rmsg, rcin, rhalf, rxin, rzs, rzin,
     lmsg, lx, lhalf, lz,
     c_send, c_recv,
@@ -112,10 +113,25 @@
     xy_device = lambda o: ((o // 4) * 4 + zh, ((o % 4) * 4 + zl) * 2 + core)
     zh_device = lambda o: (x * 4 + o, b)
     x_device = lambda o: (o * 4 + zh, b)
-    other_core = (a, b + 1 - 2 * core)
-
-    def core_copy(n, src, dst):
-        return remote(src, dst, c_send.at[n], c_recv.at[n], other_core)
+    core_device = lambda o: (a, (y * 4 + zl) * 2 + o)
+
+    def z_peer(k):
+        return (z + 8 + ((k + 1) // 2) * (2 * (k % 2) - 1) + 16) % 16
+
+    def turn(m):
+        return 2 + (m * (m + 1)) // 2
+
+    def xy_peer(k):
+        return ((x + turn(k // 4)) % 4) * 4 + (y + turn(k % 4)) % 4
+
+    def z_group(source_of, slot_of, send, recv):
+        return Group(16, z, z_device, source_of, slot_of, send, recv, z_peer)
+
+    def xy_group(source_of, slot_of, send, recv):
+        return Group(16, xy, xy_device, source_of, slot_of, send, recv, xy_peer)
+
+    def core_group(n, source_of, slot_of):
+        return Group(2, core, core_device, source_of, slot_of, c_send.at[n], c_recv.at[n])
 
     loads = [
         pltpu.make_async_copy(src, dst, in_sem.at[n])
@@ -130,15 +146,14 @@
         load.start()
     barrier = pltpu.get_barrier_semaphore()
 
-    @pl.loop(1, 16)
+    @pl.loop(0, 15)
     def _(k):
-        pl.semaphore_signal(barrier, inc=1, device_id=z_device((z + k) % 16), device_id_type=MESH)
-        pl.semaphore_signal(barrier, inc=1, device_id=xy_device((xy + k) % 16), device_id_type=MESH)
-
-    pl.semaphore_signal(barrier, inc=1, device_id=other_core, device_id_type=MESH)
+        pl.semaphore_signal(barrier, inc=1, device_id=z_device(z_peer(k)), device_id_type=MESH)
+        pl.semaphore_signal(barrier, inc=1, device_id=xy_device(xy_peer(k)), device_id_type=MESH)
+
+    pl.semaphore_signal(barrier, inc=1, device_id=core_device(1 - core), device_id_type=MESH)
     for load in loads[:5]:
         load.wait()
-
     values = al_ref[...].astype(F32)
     center = values - jnp.mean(values, -1, keepdims=True)
     inverse = lax.rsqrt(jnp.mean(center * center, -1, keepdims=True) + 1e-05)
@@ -166,7 +181,6 @@
     mask_ref[0:2, 0:RES] = w2
     lall[a, 0:32] = left.astype(BF16)
     lall[a, 32:48] = mask_ref[...].astype(BF16)
-
     loads[5].wait()
     wf[...] = w_ref[...].astype(F32)
     for d in range(WIDTH):
@@ -174,10 +188,8 @@
         wn[:, d * PAIR : (d + 1) * PAIR] = piece
         for q in range(4):
             w4[q * WIDTH : (q + 1) * WIDTH, d * PAIR : (d + 1) * PAIR] = piece
-
     pl.semaphore_wait(barrier, 31)
-
-    z_r = Group(16, z, z_device, lambda o: rsend.at[o // 4], lambda n: ra.at[n], z_r_send, z_r_recv)
+    z_r = z_group(lambda o: rsend.at[o // 4], lambda n: ra.at[n], z_r_send, z_r_recv)
     z_l = Group(
         4, zh, zh_device, lambda o: lall.at[a], lambda n: lall.at[x * 4 + n], z_l_send, z_l_recv
     )
@@ -188,7 +200,6 @@
         r, col = iota((SIZE // 8, SIZE), 0) + n * (SIZE // 8), iota((SIZE // 8, SIZE), 1)
         perm[n * (SIZE // 8) : (n + 1) * (SIZE // 8), :] = onehot(col == (r % 32) * 32 + r // 32)
     z_r.wait()
-
     r, col = iota((256, 256), 0), iota((256, 256), 1)
     order = onehot(col == ((r // 16) % 4) * 64 + ((r // 4) % 4) * 16 + (r // 64) * 4 + r % 4)
     moved = mm(order, ra[...].reshape(256, 128))
@@ -203,7 +214,7 @@
             tile = jnp.where(lanes < 64, part[2 * t], pltpu.roll(part[2 * t + 1], 64, 1))
             rb[n, t * 16 : (t + 1) * 16] = tile.astype(BF16)
         rb[n, 32:48] = masks.astype(BF16)
-    xy_r = Group(16, xy, xy_device, lambda o: rb.at[o // 4], lambda n: xr.at[core, n], xy_r_send, xy_r_recv)
+    xy_r = xy_group(lambda o: rb.at[o // 4], lambda n: xr.at[core, n], xy_r_send, xy_r_recv)
     x_l = Group(
         4, x, x_device, lambda o: lall.at[pl.ds(x * 4, 4)], lambda n: lall.at[pl.ds(n * 4, 4)],
         x_l_send, x_l_recv,
@@ -214,8 +225,7 @@
     x_l.start()
     loads[6].wait()
     xy_r.wait()
-
-    c_r = core_copy(0, xr.at[core], xr.at[core])
+    c_r = core_group(0, lambda o: xr.at[core], lambda n: xr.at[n])
     c_r.start()
     x_l.wait()
     blocks = lall[:, 0:32, :].reshape(NSEQ * 32, 128)
@@ -233,9 +243,7 @@
     masks = lall[:, 32:48, :].astype(F32)[:, 0:8, :].reshape(128, 128).astype(BF16)
     r, col = iota((128, 128), 0), iota((128, 128), 1)
     left_mask = mm(onehot((r < SEQS) & (col == (r // 2) * 8 + r % 2)), masks).astype(BF16)
-    slab = xr.at[1 - core]
-    core_copy(0, slab, slab).wait_recv()
-
+    c_r.wait()
     for c in range(2):
         for n in range(4):
             at = slice((c * 4 + n) * 16, (c * 4 + n + 1) * 16)
@@ -255,7 +263,6 @@
 
     def scale_of(step):
         return pltpu.roll(rden[...], lax.rem(128 - step * BLOCK, 128), 1)
-
     dw[...] = jnp.zeros_like(dw)
 
     @pl.loop(0, STEPS)
@@ -274,14 +281,12 @@
                         d * SEQS : (d + 1) * SEQS, h * PAIR : (h + 1) * PAIR
                     ]
         dw[...] += mm(lt[step], t_all[step])
-
     for c in range(2):
         for n in range(16):
             d = c * 16 + n
             wmsg[c, n] = dw[:, d * PAIR : (d + 1) * PAIR].astype(BF16)
-    c_w = core_copy(1, wmsg.at[1 - core], wcin)
+    c_w = core_group(1, lambda o: wmsg.at[o], lambda n: wcin)
     c_w.start()
-
     rg[...] = jnp.zeros_like(rg)
 
     def right_part(step):
@@ -298,14 +303,12 @@
         rg[...] += mm_nt(sc[step], n_all[step])
 
     pl.loop(0, 3)(right_part)
-
-    core_copy(1, wcin, wcin).wait_recv()
+    c_w.wait()
     for n in range(16):
         whalf[n] = (wmsg[core, n].astype(F32) + wcin[n].astype(F32)).astype(BF16)
-    xy_w = Group(16, xy, xy_device, lambda o: whalf.at[o], lambda n: wxin.at[n], xy_w_send, xy_w_recv)
+    xy_w = xy_group(lambda o: whalf.at[o], lambda n: wxin.at[n], xy_w_send, xy_w_recv)
     xy_w.start()
     wxin[xy] = whalf[xy]
-
     pl.loop(3, STEPS)(right_part)
     grads = mm(rg[...].astype(BF16), perm[...]).astype(BF16)
     r, col = iota((128, 128), 0), iota((128, 128), 1)
@@ -319,23 +322,21 @@
                     rmsg[c, m * 4 + n, t * 16 : (t + 1) * 16] = grads[
                         at, m * 256 + t * 128 : m * 256 + (t + 1) * 128
                     ]
-    c_g = core_copy(2, rmsg.at[1 - core], rcin)
+    c_g = core_group(2, lambda o: rmsg.at[o], lambda n: rcin)
     c_g.start()
-
     xy_w.wait()
     wz[z] = total(wxin, 0, 16).astype(BF16)
-    z_w = Group(16, z, z_device, lambda o: wz.at[z], lambda n: wz.at[n], z_w_send, z_w_recv)
+    z_w = z_group(lambda o: wz.at[z], lambda n: wz.at[n], z_w_send, z_w_recv)
     z_w.start()
-
     def left_part(step):
         rows = BLOCK * SEQS
         lgs[pl.ds(pl.multiple_of(step * rows, rows), rows), :] = mm_nt(t_all[step], w4[...])
 
     pl.loop(0, 4)(left_part)
-    core_copy(2, rcin, rcin).wait_recv()
+    c_g.wait()
     for n in range(16):
         rhalf[n] = (rmsg[core, n].astype(F32) + rcin[n].astype(F32)).astype(BF16)
-    xy_g = Group(16, xy, xy_device, lambda o: rhalf.at[o], lambda n: rxin.at[n], xy_g_send, xy_g_recv)
+    xy_g = xy_group(lambda o: rhalf.at[o], lambda n: rxin.at[n], xy_g_send, xy_g_recv)
     xy_g.start()
     rxin[xy] = rhalf[xy]
     pl.loop(4, STEPS)(left_part)
@@ -351,7 +352,6 @@
     )
     x_g.start()
     lx[x] = lmsg[pl.ds(x * 4, 4)]
-
     def pair_part(step):
         scale = scale_of(step)
         for k2 in range(BLOCK // 2):
@@ -363,7 +363,6 @@
                 ).astype(BF16)
 
     pl.loop(0, 4)(pair_part)
-
     xy_g.wait()
     sums = [total(rxin, m * 4, 4).astype(BF16) for m in range(4)]
     r, col = iota((64, 64), 0), iota((64, 64), 1)
@@ -374,24 +373,19 @@
             own = moved if h == 0 else pltpu.roll(moved, 64, 1)
             for n in range(4):
                 rzs[(2 * t + h) * 4 + n] = own[n * 16 : (n + 1) * 16].astype(BF16)
-    z_g = Group(16, z, z_device, lambda o: rzs.at[o], lambda n: rzin.at[n], z_g_send, z_g_recv)
+    z_g = z_group(lambda o: rzs.at[o], lambda n: rzin.at[n], z_g_send, z_g_recv)
     z_g.start()
     rzin[z] = rzs[z]
-
     x_g.wait()
     lhalf[...] = total(lx, 0, 4).astype(BF16)
     zl_g = Group(4, zh, zh_device, lambda o: lhalf.at[o], lambda n: lz.at[n], zl_g_send, zl_g_recv)
     zl_g.start()
     lz[zh] = lhalf[zh]
-
     z_w.wait()
     fin[core, xy] = total(wz, 0, 16).astype(BF16)
-    xy_f = Group(
-        16, xy, xy_device, lambda o: fin.at[core, xy], lambda n: fin.at[core, n], xy_f_send, xy_f_recv
-    )
+    xy_f = xy_group(lambda o: fin.at[core, xy], lambda n: fin.at[core, n], xy_f_send, xy_f_recv)
     xy_f.start()
     pl.loop(4, STEPS)(pair_part)
-
     values = al_ref[...].astype(F32)
     center = values - jnp.mean(values, -1, keepdims=True)
     inverse = lax.rsqrt(jnp.mean(center * center, -1, keepdims=True) + 1e-05)
@@ -417,32 +411,45 @@
         first = jnp.mean(grad, -1, keepdims=True)
         second = jnp.mean(grad * normal[span], -1, keepdims=True)
         ag_ref[span] = (inverse[span] * (grad - first - normal[span] * second)).astype(BF16)
-
     xy_f.wait()
-    c_f = core_copy(3, fin.at[core], fin.at[core])
+    c_f = core_group(3, lambda o: fin.at[core], lambda n: fin.at[n])
     c_f.start()
-    for group in (z_r, z_l, xy_r, x_l, xy_w, z_w, xy_f, xy_g, z_g, x_g, zl_g):
+    for group in (z_r, z_l, xy_r, x_l, c_r, c_w, c_g, xy_w, z_w, xy_f, xy_g, z_g, x_g, zl_g, c_f):
         group.sent()
-    for copy in (c_r, c_w, c_g, c_f):
-        copy.wait_send()
-    slab = fin.at[1 - core]
-    core_copy(3, slab, slab).wait_recv()
+    c_f.wait()
+
+
+def write_kernel(pair_in, ag_in, fin_ref, pair_out, ag_out, dw_out, dw_ref, sem):
+    parts = [
+        pltpu.make_async_copy(pair_in.at[pl.ds(n * 8, 8)], pair_out.at[pl.ds(n * 8, 8)], sem.at[2 + n])
+        for n in range(8)
+    ]
+    for part in parts:
+        part.start()
+    rows = pltpu.make_async_copy(ag_in, ag_out, sem.at[0])
+    rows.start()
     for c in range(2):
         for n in range(16):
-            dw_ref[pl.ds(c * 16 + n, WIDTH, stride=WIDTH), :] = fin[c, n].astype(F32)
+            dw_ref[pl.ds(c * 16 + n, WIDTH, stride=WIDTH), :] = fin_ref[c, n].astype(F32)
+    grads = pltpu.make_async_copy(dw_ref, dw_out, sem.at[1])
+    grads.start()
+    for part in parts:
+        part.wait()
+    rows.wait()
+    grads.wait()
 
 
 def shards(alignment, align_mask, residue_mask, left_weight, right_weight, out_weight, pair_cotangent):
     dma = pltpu.SemaphoreType.DMA
     vmem = pltpu.VMEM
-    pair, ag, dw = pl.pallas_call(
+    pair, ag, fin = pl.pallas_call(
         kernel,
         out_shape=(
             jax.ShapeDtypeStruct((RES, COLS, PAIR), BF16),
             jax.ShapeDtypeStruct((2 * RES, CH), BF16),
-            jax.ShapeDtypeStruct((SIZE, PAIR), F32),
+            jax.ShapeDtypeStruct((2, 16, WIDTH, PAIR), BF16),
         ),
-        in_specs=[pl.BlockSpec(memory_space=pl.ANY)] * 7,
+        in_specs=[pl.BlockSpec(memory_space=pltpu.HBM)] * 7,
         out_specs=(pl.BlockSpec(memory_space=pltpu.VMEM),) * 3,
         scratch_shapes=[
             vmem((2 * RES, CH), BF16), vmem((2, RES), jnp.int32), vmem((1, RES), jnp.int32),
@@ -459,24 +466,38 @@
             vmem((STEPS, COLS, BLOCK * PAIR), BF16), vmem((COLS, SIZE), F32),
             vmem((RES * SEQS, 128), F32), vmem((WIDTH, WIDTH * PAIR), F32),
             vmem((2, 16, 32, 128), BF16), vmem((16, 32, 128), BF16), vmem((16, 32, 128), BF16),
-            vmem((16, 32, 128), BF16), vmem((16, 32, 128), BF16), vmem((2, 16, 32, 128), BF16),
+            vmem((16, 32, 128), BF16), vmem((16, 32, 128), BF16),
             vmem((2, 16, 32, 128), BF16), vmem((16, 32, 128), BF16), vmem((16, 32, 128), BF16),
             vmem((16, 32, 128), BF16), vmem((16, 16, 128), BF16), vmem((16, 16, 128), BF16),
             vmem((NSEQ, 32, 128), BF16), vmem((4, 4, 32, 128), BF16), vmem((4, 32, 128), BF16),
             vmem((4, 32, 128), BF16),
-            dma((4,)), dma((4,)),
+            dma((4, 2)), dma((4, 2)),
             dma((16,)), dma((16,)), dma((4,)), dma((4,)), dma((16,)), dma((16,)), dma((4,)), dma((4,)),
             dma((16,)), dma((16,)), dma((16,)), dma((16,)), dma((16,)), dma((16,)),
             dma((16,)), dma((16,)), dma((16,)), dma((16,)), dma((4,)), dma((4,)), dma((4,)), dma((4,)),
         ],
         compiler_params=pltpu.CompilerParams(
-            collective_id=0, has_side_effects=True, vmem_limit_bytes=58 * 1024 * 1024
+            collective_id=0, has_side_effects=True, vmem_limit_bytes=60000000
         ),
         name="pair_update",
     )(
         alignment.reshape(2 * RES, CH), align_mask, residue_mask.reshape(1, RES), left_weight.T, right_weight.T,
         out_weight, pair_cotangent.reshape(RES, COLS, PAIR),
     )
+    anywhere = pl.BlockSpec(memory_space=pl.ANY)
+    pair, ag, dw = pl.pallas_call(
+        write_kernel,
+        out_shape=(
+            jax.ShapeDtypeStruct((RES, COLS, PAIR), BF16),
+            jax.ShapeDtypeStruct((2 * RES, CH), BF16),
+            jax.ShapeDtypeStruct((SIZE, PAIR), F32),
+        ),
+        in_specs=[anywhere, anywhere, pl.BlockSpec(memory_space=pltpu.VMEM)],
+        out_specs=(anywhere, anywhere, anywhere),
+        scratch_shapes=[vmem((SIZE, PAIR), F32), dma((10,))],
+        compiler_params=pltpu.CompilerParams(vmem_limit_bytes=60000000),
+        name="write_outputs",
+    )(pair, ag, fin)
     return pair.reshape(pair_cotangent.shape), ag.reshape(alignment.shape), dw
 
 

time: 90.9 us -> 153 us (1.68)
  Pallas kernels: 84.1 us -> 152 us
  local copies, waits for them, and re-layouts: 5.96 us -> 0 us
    pallas_call x0 -> x1, Pallas kernels: none -> 67.7 us  [shards(): pl.pallas_call(write_kernel, out_shape=(jax.ShapeDtypeStruct((RES, COLS,...]
    unnamed x7 -> x0, local copies, waits for them, and re-layouts: 5.96 us -> none
where the time goes in v3:
time: 153 us; the launch traced here: 152 us
  Pallas kernels  152 us (99%)
    pallas_call x1, Pallas kernels, shards(): pl.pallas_call(kernel, out_shape=(jax.ShapeDtypeStruct((RES, COLS, PAIR),...  84.1 us
    pallas_call x1, Pallas kernels, shards(): pl.pallas_call(write_kernel, out_shape=(jax.ShapeDtypeStruct((RES, COLS,...  67.7 us

profile of v3, /device:TPU:1, one launch (start us, length us, event | category | flops | bytes accessed | tf_op | source)
XLA Modules:
  0.0 152.4 jit_solution(5428392028994305189)
XLA Ops:
  0.6 84.1 %pair_update.1 = (bf16[64,128,128]{2,1,0:T(8,128)(2,1)}, bf16[128,256]{1,0:T(8,128)(2,1)}, bf16[2,16,32,128]{3,2,1,0:T(8,128)(2,1)}) custom-call(bf16[128,256]{1,0:T(8,128)(2,1)} %bitcast.8, s32[2,64]{1,0:T(2,128)} %am_hbm.1, s32[1,64]{1,0:T(1,128)} %bitcast.11, bf16[32,256]{1,0:T(8,128)(2,1)} %bitcast.9, bf16[32,256]{1,0:T(8,128)(2,1)} %bitcast.10, ...), custom_call_target="tpu_custom_call" | custom-call | tf_op jit(solution)/shard_map/pair_update/pallas_call | solution.py:445
  84.8 67.7 %write_outputs.1 = (bf16[64,128,128]{2,1,0:T(8,128)(2,1)}, bf16[128,256]{1,0:T(8,128)(2,1)}, f32[1024,128]{1,0:T(8,128)}) custom-call(bf16[64,128,128]{2,1,0:T(8,128)(2,1)} %get-tuple-element.9.pair_in, bf16[128,256]{1,0:T(8,128)(2,1)} %get-tuple-element.10.ag_in, bf16[2,16,32,128]{3,2,1,0:T(8,128)(2,1)} %get-tuple-element.11.fin_ref), custom_call_target="tpu_custom_call" | custom-call | tf_op jit(solution)/shard_map/write_outputs/pallas_call | solution.py:488

commit v4 on v3

--- a/solution.py
+++ b/solution.py
@@ -12,6 +12,7 @@
 NSEQ, SEQS, RES, WIDTH, CH, PAIR, COLS = 16, 32, 64, 32, 256, 128, 128
 BLOCK = 8
 STEPS = RES // BLOCK
+EARLY = 4
 SIZE = WIDTH * SEQS
 NT_DIMS = (((1,), (1,)), ((), ()))
 
@@ -93,10 +94,10 @@
 
 def kernel(
     al_hbm, am_hbm, rm_hbm, wl_hbm, wr_hbm, w_hbm, ct_hbm,
-    pair_ref, ag_ref, fin,
+    pair_hbm, ag_ref, fin,
     al_ref, am_ref, rm_ref, wl_ref, wr_ref, w_ref, ct_ref, in_sem,
     mask_ref, rsend, ra, rb, xr, lall,
-    wf, wn, w4, lf, l2, lt, perm, rp, rm_all, rds, rt, rden, n_all, t_all, sc, rg, lgs, dw,
+    wf, wn, w4, lf, l2, lt, perm, rp, rm_all, rds, rt, rden, n_all, t_all, sc, rg, lgs, dw, pair_ref, pair_sem,
     wmsg, wcin, whalf, wxin, wz,
     rmsg, rcin, rhalf, rxin, rzs, rzin,
     lmsg, lx, lhalf, lz,
@@ -199,7 +200,14 @@
     for n in range(8):
         r, col = iota((SIZE // 8, SIZE), 0) + n * (SIZE // 8), iota((SIZE // 8, SIZE), 1)
         perm[n * (SIZE // 8) : (n + 1) * (SIZE // 8), :] = onehot(col == (r % 32) * 32 + r // 32)
+    z_l.wait()
+    x_l = Group(
+        4, x, x_device, lambda o: lall.at[pl.ds(x * 4, 4)], lambda n: lall.at[pl.ds(n * 4, 4)],
+        x_l_send, x_l_recv,
+    )
+    x_l.start()
     z_r.wait()
+
     r, col = iota((256, 256), 0), iota((256, 256), 1)
     order = onehot(col == ((r // 16) % 4) * 64 + ((r // 4) % 4) * 16 + (r // 64) * 4 + r % 4)
     moved = mm(order, ra[...].reshape(256, 128))
@@ -215,18 +223,9 @@
             rb[n, t * 16 : (t + 1) * 16] = tile.astype(BF16)
         rb[n, 32:48] = masks.astype(BF16)
     xy_r = xy_group(lambda o: rb.at[o // 4], lambda n: xr.at[core, n], xy_r_send, xy_r_recv)
-    x_l = Group(
-        4, x, x_device, lambda o: lall.at[pl.ds(x * 4, 4)], lambda n: lall.at[pl.ds(n * 4, 4)],
-        x_l_send, x_l_recv,
-    )
     xy_r.start()
     xr[core, xy] = rb[x]
-    z_l.wait()
-    x_l.start()
     loads[6].wait()
-    xy_r.wait()
-    c_r = core_group(0, lambda o: xr.at[core], lambda n: xr.at[n])
-    c_r.start()
     x_l.wait()
     blocks = lall[:, 0:32, :].reshape(NSEQ * 32, 128)
     row, lane = iota((128, 128), 0), iota((128, 128), 1)
@@ -243,6 +242,22 @@
     masks = lall[:, 32:48, :].astype(F32)[:, 0:8, :].reshape(128, 128).astype(BF16)
     r, col = iota((128, 128), 0), iota((128, 128), 1)
     left_mask = mm(onehot((r < SEQS) & (col == (r // 2) * 8 + r % 2)), masks).astype(BF16)
+    xy_r.wait()
+    c_r = core_group(0, lambda o: xr.at[core], lambda n: xr.at[n])
+    c_r.start()
+    def n_part(step):
+        rows = BLOCK * SEQS
+        l2c = l2[pl.ds(pl.multiple_of(step * rows, rows), rows), 0:WIDTH]
+        for d2 in range(WIDTH // 2):
+            part = mm(l2c, wn[:, d2 * 256 : (d2 + 1) * 256]).astype(BF16)
+            for h in range(2):
+                d = 2 * d2 + h
+                for k in range(BLOCK):
+                    n_all[step, d * SEQS : (d + 1) * SEQS, k * PAIR : (k + 1) * PAIR] = part[
+                        k * SEQS : (k + 1) * SEQS, h * PAIR : (h + 1) * PAIR
+                    ]
+
+    pl.loop(0, EARLY)(n_part)
     c_r.wait()
     for c in range(2):
         for n in range(4):
@@ -290,26 +305,19 @@
     rg[...] = jnp.zeros_like(rg)
 
     def right_part(step):
-        rows = BLOCK * SEQS
-        l2c = l2[pl.ds(pl.multiple_of(step * rows, rows), rows), 0:WIDTH]
-        for d2 in range(WIDTH // 2):
-            part = mm(l2c, wn[:, d2 * 256 : (d2 + 1) * 256]).astype(BF16)
-            for h in range(2):
-                d = 2 * d2 + h
-                for k in range(BLOCK):
-                    n_all[step, d * SEQS : (d + 1) * SEQS, k * PAIR : (k + 1) * PAIR] = part[
-                        k * SEQS : (k + 1) * SEQS, h * PAIR : (h + 1) * PAIR
-                    ]
         rg[...] += mm_nt(sc[step], n_all[step])
 
-    pl.loop(0, 3)(right_part)
+    pl.loop(0, EARLY)(right_part)
     c_w.wait()
     for n in range(16):
         whalf[n] = (wmsg[core, n].astype(F32) + wcin[n].astype(F32)).astype(BF16)
     xy_w = xy_group(lambda o: whalf.at[o], lambda n: wxin.at[n], xy_w_send, xy_w_recv)
     xy_w.start()
     wxin[xy] = whalf[xy]
-    pl.loop(3, STEPS)(right_part)
+    @pl.loop(EARLY, STEPS)
+    def _(step):
+        n_part(step)
+        right_part(step)
     grads = mm(rg[...].astype(BF16), perm[...]).astype(BF16)
     r, col = iota((128, 128), 0), iota((128, 128), 1)
     order = onehot(col == ((r // 16) % 4) * 32 + ((r // 4) % 4) * 8 + (r // 64) * 4 + r % 4)
@@ -362,7 +370,12 @@
                     part[:, h * PAIR : (h + 1) * PAIR] * scale[:, k : k + 1]
                 ).astype(BF16)
 
+    def pair_copy(n):
+        span = pl.ds(n * (RES // 2), RES // 2)
+        return pltpu.make_async_copy(pair_ref.at[span], pair_hbm.at[span], pair_sem.at[n])
+
     pl.loop(0, 4)(pair_part)
+    pair_copy(0).start()
     xy_g.wait()
     sums = [total(rxin, m * 4, 4).astype(BF16) for m in range(4)]
     r, col = iota((64, 64), 0), iota((64, 64), 1)
@@ -386,6 +399,7 @@
     xy_f = xy_group(lambda o: fin.at[core, xy], lambda n: fin.at[core, n], xy_f_send, xy_f_recv)
     xy_f.start()
     pl.loop(4, STEPS)(pair_part)
+    pair_copy(1).start()
     values = al_ref[...].astype(F32)
     center = values - jnp.mean(values, -1, keepdims=True)
     inverse = lax.rsqrt(jnp.mean(center * center, -1, keepdims=True) + 1e-05)
@@ -416,27 +430,37 @@
     c_f.start()
     for group in (z_r, z_l, xy_r, x_l, c_r, c_w, c_g, xy_w, z_w, xy_f, xy_g, z_g, x_g, zl_g, c_f):
         group.sent()
+    for n in range(2):
+        pair_copy(n).wait()
     c_f.wait()
 
 
-def write_kernel(pair_in, ag_in, fin_ref, pair_out, ag_out, dw_out, dw_ref, sem):
-    parts = [
-        pltpu.make_async_copy(pair_in.at[pl.ds(n * 8, 8)], pair_out.at[pl.ds(n * 8, 8)], sem.at[2 + n])
-        for n in range(8)
+def write_kernel(pair_in, ag_in, fin_in, pair_out, ag_out, dw_out, pair_ref, ag_ref, fin_ref, dw_ref, sem, out_sem):
+    count = 8
+    rows = RES // count
+    ins = [
+        pltpu.make_async_copy(fin_in, fin_ref, sem.at[0]),
+        pltpu.make_async_copy(ag_in, ag_ref, sem.at[1]),
     ]
-    for part in parts:
-        part.start()
-    rows = pltpu.make_async_copy(ag_in, ag_out, sem.at[0])
-    rows.start()
-    for c in range(2):
-        for n in range(16):
-            dw_ref[pl.ds(c * 16 + n, WIDTH, stride=WIDTH), :] = fin_ref[c, n].astype(F32)
-    grads = pltpu.make_async_copy(dw_ref, dw_out, sem.at[1])
-    grads.start()
-    for part in parts:
-        part.wait()
-    rows.wait()
-    grads.wait()
+    outs = [
+        pltpu.make_async_copy(dw_ref, dw_out, out_sem.at[0]),
+        pltpu.make_async_copy(ag_ref, ag_out, out_sem.at[1]),
+    ]
+    for n in range(count):
+        span = pl.ds(n * rows, rows)
+        ins.append(pltpu.make_async_copy(pair_in.at[span], pair_ref.at[span], sem.at[2 + n]))
+        outs.append(pltpu.make_async_copy(pair_ref.at[span], pair_out.at[span], out_sem.at[2 + n]))
+    for copy in ins:
+        copy.start()
+    for n, copy in enumerate(ins):
+        copy.wait()
+        if n == 0:
+            for c in range(2):
+                for d in range(16):
+                    dw_ref[pl.ds(c * 16 + d, WIDTH, stride=WIDTH), :] = fin_ref[c, d].astype(F32)
+        outs[n].start()
+    for copy in outs:
+        copy.wait()
 
 
 def shards(alignment, align_mask, residue_mask, left_weight, right_weight, out_weight, pair_cotangent):
@@ -450,7 +474,7 @@
             jax.ShapeDtypeStruct((2, 16, WIDTH, PAIR), BF16),
         ),
         in_specs=[pl.BlockSpec(memory_space=pltpu.HBM)] * 7,
-        out_specs=(pl.BlockSpec(memory_space=pltpu.VMEM),) * 3,
+        out_specs=(pl.BlockSpec(memory_space=pl.ANY),) + (pl.BlockSpec(memory_space=pltpu.VMEM),) * 2,
         scratch_shapes=[
             vmem((2 * RES, CH), BF16), vmem((2, RES), jnp.int32), vmem((1, RES), jnp.int32),
             vmem((WIDTH, CH), BF16), vmem((WIDTH, CH), BF16), vmem((SIZE, PAIR), BF16),
@@ -465,6 +489,7 @@
             vmem((STEPS, SIZE, BLOCK * PAIR), BF16), vmem((STEPS, BLOCK * SEQS, WIDTH * PAIR), BF16),
             vmem((STEPS, COLS, BLOCK * PAIR), BF16), vmem((COLS, SIZE), F32),
             vmem((RES * SEQS, 128), F32), vmem((WIDTH, WIDTH * PAIR), F32),
+            vmem((RES, COLS, PAIR), BF16), dma((2,)),
             vmem((2, 16, 32, 128), BF16), vmem((16, 32, 128), BF16), vmem((16, 32, 128), BF16),
             vmem((16, 32, 128), BF16), vmem((16, 32, 128), BF16),
             vmem((2, 16, 32, 128), BF16), vmem((16, 32, 128), BF16), vmem((16, 32, 128), BF16),
@@ -492,9 +517,12 @@
             jax.ShapeDtypeStruct((2 * RES, CH), BF16),
             jax.ShapeDtypeStruct((SIZE, PAIR), F32),
         ),
-        in_specs=[anywhere, anywhere, pl.BlockSpec(memory_space=pltpu.VMEM)],
+        in_specs=[anywhere] * 3,
         out_specs=(anywhere, anywhere, anywhere),
-        scratch_shapes=[vmem((SIZE, PAIR), F32), dma((10,))],
+        scratch_shapes=[
+            vmem((RES, COLS, PAIR), BF16), vmem((2 * RES, CH), BF16), vmem((2, 16, WIDTH, PAIR), BF16),
+            vmem((SIZE, PAIR), F32), dma((10,)), dma((10,)),
+        ],
         compiler_params=pltpu.CompilerParams(vmem_limit_bytes=60000000),
         name="write_outputs",
     )(pair, ag, fin)

time: 153 us -> 87.9 us (0.57)
  Pallas kernels: 152 us -> 87.1 us
    pallas_call x1, Pallas kernels: 67.7 us -> 3.11 us  [shards(): pl.pallas_call(write_kernel, out_shape=(jax.ShapeDtypeStruct((RES, COLS,...]
where the time goes in v4:
time: 87.9 us; the launch traced here: 87.7 us
  Pallas kernels  87.1 us (99%)
    pallas_call x1, Pallas kernels, shards(): pl.pallas_call(kernel, out_shape=(jax.ShapeDtypeStruct((RES, COLS, PAIR),...  84 us
    pallas_call x1, Pallas kernels, shards(): pl.pallas_call(write_kernel, out_shape=(jax.ShapeDtypeStruct((RES, COLS,...  3.11 us

profile of v4, /device:TPU:1, one launch (start us, length us, event | category | flops | bytes accessed | tf_op | source)
XLA Modules:
  0.0 87.7 jit_solution(4006561077219996075)
XLA Ops:
  0.6 84.0 %pair_update.1 = (bf16[64,128,128]{2,1,0:T(8,128)(2,1)}, bf16[128,256]{1,0:T(8,128)(2,1)}, bf16[2,16,32,128]{3,2,1,0:T(8,128)(2,1)}) custom-call(bf16[128,256]{1,0:T(8,128)(2,1)} %bitcast.8, s32[2,64]{1,0:T(2,128)} %am_hbm.1, s32[1,64]{1,0:T(1,128)} %bitcast.11, bf16[32,256]{1,0:T(8,128)(2,1)} %bitcast.9, bf16[32,256]{1,0:T(8,128)(2,1)} %bitcast.10, ...), custom_call_target="tpu_custom_call" | custom-call | tf_op jit(solution)/shard_map/pair_update/pallas_call | solution.py:469
  84.6 3.1 %write_outputs.1 = (bf16[64,128,128]{2,1,0:T(8,128)(2,1)}, bf16[128,256]{1,0:T(8,128)(2,1)}, f32[1024,128]{1,0:T(8,128)}) custom-call(bf16[64,128,128]{2,1,0:T(8,128)(2,1)} %get-tuple-element.9.pair_in, bf16[128,256]{1,0:T(8,128)(2,1)} %get-tuple-element.10.ag_in, bf16[2,16,32,128]{3,2,1,0:T(8,128)(2,1)} %get-tuple-element.11.fin_in), custom_call_target="tpu_custom_call" | custom-call | tf_op jit(solution)/shard_map/write_outputs/pallas_call | solution.py:513

commit v5 on v4

--- a/solution.py
+++ b/solution.py
@@ -143,8 +143,6 @@
             )
         )
     ]
-    for load in loads:
-        load.start()
     barrier = pltpu.get_barrier_semaphore()
 
     @pl.loop(0, 15)
@@ -153,6 +151,8 @@
         pl.semaphore_signal(barrier, inc=1, device_id=xy_device(xy_peer(k)), device_id_type=MESH)
 
     pl.semaphore_signal(barrier, inc=1, device_id=core_device(1 - core), device_id_type=MESH)
+    for load in loads:
+        load.start()
     for load in loads[:5]:
         load.wait()
     values = al_ref[...].astype(F32)
@@ -246,8 +246,7 @@
     c_r = core_group(0, lambda o: xr.at[core], lambda n: xr.at[n])
     c_r.start()
     def n_part(step):
-        rows = BLOCK * SEQS
-        l2c = l2[pl.ds(pl.multiple_of(step * rows, rows), rows), 0:WIDTH]
+        l2c = l2[step * rows : (step + 1) * rows, 0:WIDTH]
         for d2 in range(WIDTH // 2):
             part = mm(l2c, wn[:, d2 * 256 : (d2 + 1) * 256]).astype(BF16)
             for h in range(2):
@@ -257,7 +256,8 @@
                         k * SEQS : (k + 1) * SEQS, h * PAIR : (h + 1) * PAIR
                     ]
 
-    pl.loop(0, EARLY)(n_part)
+    for step in range(EARLY):
+        n_part(step)
     c_r.wait()
     for c in range(2):
         for n in range(4):
@@ -277,11 +277,10 @@
     rt[...] = mm_nt(perm[...], right).astype(BF16)
 
     def scale_of(step):
-        return pltpu.roll(rden[...], lax.rem(128 - step * BLOCK, 128), 1)
+        return pltpu.roll(rden[...], (128 - step * BLOCK) % 128, 1)
     dw[...] = jnp.zeros_like(dw)
 
-    @pl.loop(0, STEPS)
-    def _(step):
+    def t_part(step):
         scale = scale_of(step)
         for k in range(BLOCK):
             sc[step, :, k * PAIR : (k + 1) * PAIR] = (
@@ -295,7 +294,12 @@
                     t_all[step, k * SEQS : (k + 1) * SEQS, d * PAIR : (d + 1) * PAIR] = part[
                         d * SEQS : (d + 1) * SEQS, h * PAIR : (h + 1) * PAIR
                     ]
-        dw[...] += mm(lt[step], t_all[step])
+
+    for step in range(STEPS + 1):
+        if step < STEPS:
+            t_part(step)
+        if step > 0:
+            dw[...] += mm(lt[step - 1], t_all[step - 1])
     for c in range(2):
         for n in range(16):
             d = c * 16 + n
@@ -305,23 +309,24 @@
     rg[...] = jnp.zeros_like(rg)
 
     def right_part(step):
-        rg[...] += mm_nt(sc[step], n_all[step])
-
-    pl.loop(0, EARLY)(right_part)
+        rg[...] += mm_nt(n_all[step], sc[step])
+
+    for step in range(EARLY):
+        right_part(step)
     c_w.wait()
     for n in range(16):
         whalf[n] = (wmsg[core, n].astype(F32) + wcin[n].astype(F32)).astype(BF16)
     xy_w = xy_group(lambda o: whalf.at[o], lambda n: wxin.at[n], xy_w_send, xy_w_recv)
     xy_w.start()
     wxin[xy] = whalf[xy]
-    @pl.loop(EARLY, STEPS)
-    def _(step):
+    for step in range(EARLY, STEPS):
         n_part(step)
+    for step in range(EARLY, STEPS):
         right_part(step)
-    grads = mm(rg[...].astype(BF16), perm[...]).astype(BF16)
     r, col = iota((128, 128), 0), iota((128, 128), 1)
     order = onehot(col == ((r // 16) % 4) * 32 + ((r // 4) % 4) * 8 + (r // 64) * 4 + r % 4)
-    grads = mm(order, grads).astype(BF16)
+    grads = mm_nt(order, rg[...].astype(BF16)).astype(BF16)
+    grads = mm(grads, perm[...]).astype(BF16)
     for c in range(2):
         for m in range(4):
             for n in range(4):
@@ -336,18 +341,19 @@
     wz[z] = total(wxin, 0, 16).astype(BF16)
     z_w = z_group(lambda o: wz.at[z], lambda n: wz.at[n], z_w_send, z_w_recv)
     z_w.start()
-    def left_part(step):
-        rows = BLOCK * SEQS
-        lgs[pl.ds(pl.multiple_of(step * rows, rows), rows), :] = mm_nt(t_all[step], w4[...])
-
-    pl.loop(0, 4)(left_part)
+    def left_part(n):
+        blocks = t_all[2 * n : 2 * n + 2].reshape(2 * rows, WIDTH * PAIR)
+        lgs[n * 2 * rows : (n + 1) * 2 * rows, :] = mm_nt(blocks, w4[...])
+
+    left_part(0)
     c_g.wait()
     for n in range(16):
         rhalf[n] = (rmsg[core, n].astype(F32) + rcin[n].astype(F32)).astype(BF16)
     xy_g = xy_group(lambda o: rhalf.at[o], lambda n: rxin.at[n], xy_g_send, xy_g_recv)
     xy_g.start()
     rxin[xy] = rhalf[xy]
-    pl.loop(4, STEPS)(left_part)
+    for n in range(1, STEPS // 2):
+        left_part(n)
     lane = iota((32, 128), 1) // WIDTH
     for n in range(NSEQ):
         out = lgs[pl.ds(2 * n, 32, stride=SEQS), :]
@@ -374,8 +380,11 @@
         span = pl.ds(n * (RES // 2), RES // 2)
         return pltpu.make_async_copy(pair_ref.at[span], pair_hbm.at[span], pair_sem.at[n])
 
-    pl.loop(0, 4)(pair_part)
-    pair_copy(0).start()
+    for step in range(STEPS):
+        pair_part(step)
+        if step == STEPS // 2 - 1:
+            pair_copy(0).start()
+    pair_copy(1).start()
     xy_g.wait()
     sums = [total(rxin, m * 4, 4).astype(BF16) for m in range(4)]
     r, col = iota((64, 64), 0), iota((64, 64), 1)
@@ -398,8 +407,6 @@
     fin[core, xy] = total(wz, 0, 16).astype(BF16)
     xy_f = xy_group(lambda o: fin.at[core, xy], lambda n: fin.at[core, n], xy_f_send, xy_f_recv)
     xy_f.start()
-    pl.loop(4, STEPS)(pair_part)
-    pair_copy(1).start()
     values = al_ref[...].astype(F32)
     center = values - jnp.mean(values, -1, keepdims=True)
     inverse = lax.rsqrt(jnp.mean(center * center, -1, keepdims=True) + 1e-05)
@@ -487,7 +494,7 @@
             vmem((COLS, SIZE), BF16), vmem((COLS, 128), F32), vmem((COLS, SIZE), BF16),
             vmem((SIZE, COLS), BF16), vmem((COLS, 128), F32),
             vmem((STEPS, SIZE, BLOCK * PAIR), BF16), vmem((STEPS, BLOCK * SEQS, WIDTH * PAIR), BF16),
-            vmem((STEPS, COLS, BLOCK * PAIR), BF16), vmem((COLS, SIZE), F32),
+            vmem((STEPS, COLS, BLOCK * PAIR), BF16), vmem((SIZE, COLS), F32),
             vmem((RES * SEQS, 128), F32), vmem((WIDTH, WIDTH * PAIR), F32),
             vmem((RES, COLS, PAIR), BF16), dma((2,)),
             vmem((2, 16, 32, 128), BF16), vmem((16, 32, 128), BF16), vmem((16, 32, 128), BF16),

time: 87.9 us -> 88 us (level)
  no operation moved by 1% of the time
where the time goes in v5:
time: 88 us; the launch traced here: 87.8 us
  Pallas kernels  87 us (99%)
    pallas_call x1, Pallas kernels, shards(): pl.pallas_call(kernel, out_shape=(jax.ShapeDtypeStruct((RES, COLS, PAIR),...  83.9 us
    pallas_call x1, Pallas kernels, shards(): pl.pallas_call(write_kernel, out_shape=(jax.ShapeDtypeStruct((RES, COLS,...  3.11 us

profile of v5, /device:TPU:1, one launch (start us, length us, event | category | flops | bytes accessed | tf_op | source)
XLA Modules:
  0.0 87.8 jit_solution(9873825186083542343)
XLA Ops:
  0.6 83.9 %pair_update.1 = (bf16[64,128,128]{2,1,0:T(8,128)(2,1)}, bf16[128,256]{1,0:T(8,128)(2,1)}, bf16[2,16,32,128]{3,2,1,0:T(8,128)(2,1)}) custom-call(bf16[128,256]{1,0:T(8,128)(2,1)} %bitcast.8, s32[2,64]{1,0:T(2,128)} %am_hbm.1, s32[1,64]{1,0:T(1,128)} %bitcast.11, bf16[32,256]{1,0:T(8,128)(2,1)} %bitcast.9, bf16[32,256]{1,0:T(8,128)(2,1)} %bitcast.10, ...), custom_call_target="tpu_custom_call" | custom-call | tf_op jit(solution)/shard_map/pair_update/pallas_call | solution.py:476
  84.5 3.1 %write_outputs.1 = (bf16[64,128,128]{2,1,0:T(8,128)(2,1)}, bf16[128,256]{1,0:T(8,128)(2,1)}, f32[1024,128]{1,0:T(8,128)}) custom-call(bf16[64,128,128]{2,1,0:T(8,128)(2,1)} %get-tuple-element.9.pair_in, bf16[128,256]{1,0:T(8,128)(2,1)} %get-tuple-element.10.ag_in, bf16[2,16,32,128]{3,2,1,0:T(8,128)(2,1)} %get-tuple-element.11.fin_in), custom_call_target="tpu_custom_call" | custom-call | tf_op jit(solution)/shard_map/write_outputs/pallas_call | solution.py:520

commit v6 on v5

--- a/solution.py
+++ b/solution.py
@@ -337,15 +337,15 @@
                     ]
     c_g = core_group(2, lambda o: rmsg.at[o], lambda n: rcin)
     c_g.start()
+    def left_part(n):
+        blocks = t_all[2 * n : 2 * n + 2].reshape(2 * rows, WIDTH * PAIR)
+        lgs[n * 2 * rows : (n + 1) * 2 * rows, :] = mm_nt(blocks, w4[...])
+
+    left_part(0)
     xy_w.wait()
     wz[z] = total(wxin, 0, 16).astype(BF16)
     z_w = z_group(lambda o: wz.at[z], lambda n: wz.at[n], z_w_send, z_w_recv)
     z_w.start()
-    def left_part(n):
-        blocks = t_all[2 * n : 2 * n + 2].reshape(2 * rows, WIDTH * PAIR)
-        lgs[n * 2 * rows : (n + 1) * 2 * rows, :] = mm_nt(blocks, w4[...])
-
-    left_part(0)
     c_g.wait()
     for n in range(16):
         rhalf[n] = (rmsg[core, n].astype(F32) + rcin[n].astype(F32)).astype(BF16)
@@ -366,25 +366,6 @@
     )
     x_g.start()
     lx[x] = lmsg[pl.ds(x * 4, 4)]
-    def pair_part(step):
-        scale = scale_of(step)
-        for k2 in range(BLOCK // 2):
-            part = mm(rds[...], n_all[step, :, k2 * 256 : (k2 + 1) * 256])
-            for h in range(2):
-                k = 2 * k2 + h
-                pair_ref[step * BLOCK + k] = (
-                    part[:, h * PAIR : (h + 1) * PAIR] * scale[:, k : k + 1]
-                ).astype(BF16)
-
-    def pair_copy(n):
-        span = pl.ds(n * (RES // 2), RES // 2)
-        return pltpu.make_async_copy(pair_ref.at[span], pair_hbm.at[span], pair_sem.at[n])
-
-    for step in range(STEPS):
-        pair_part(step)
-        if step == STEPS // 2 - 1:
-            pair_copy(0).start()
-    pair_copy(1).start()
     xy_g.wait()
     sums = [total(rxin, m * 4, 4).astype(BF16) for m in range(4)]
     r, col = iota((64, 64), 0), iota((64, 64), 1)
@@ -398,20 +379,52 @@
     z_g = z_group(lambda o: rzs.at[o], lambda n: rzin.at[n], z_g_send, z_g_recv)
     z_g.start()
     rzin[z] = rzs[z]
+    z_w.wait()
+    fin[core, xy] = total(wz, 0, 16).astype(BF16)
+    xy_f = xy_group(lambda o: fin.at[core, xy], lambda n: fin.at[core, n], xy_f_send, xy_f_recv)
+    xy_f.start()
     x_g.wait()
     lhalf[...] = total(lx, 0, 4).astype(BF16)
     zl_g = Group(4, zh, zh_device, lambda o: lhalf.at[o], lambda n: lz.at[n], zl_g_send, zl_g_recv)
     zl_g.start()
     lz[zh] = lhalf[zh]
-    z_w.wait()
-    fin[core, xy] = total(wz, 0, 16).astype(BF16)
-    xy_f = xy_group(lambda o: fin.at[core, xy], lambda n: fin.at[core, n], xy_f_send, xy_f_recv)
-    xy_f.start()
+
+    def pair_part(step):
+        scale = scale_of(step)
+        for k2 in range(BLOCK // 2):
+            part = mm(rds[...], n_all[step, :, k2 * 256 : (k2 + 1) * 256])
+            for h in range(2):
+                k = 2 * k2 + h
+                pair_ref[step * BLOCK + k] = (
+                    part[:, h * PAIR : (h + 1) * PAIR] * scale[:, k : k + 1]
+                ).astype(BF16)
+
+    def pair_copy(n):
+        span = pl.ds(n * (RES // 2), RES // 2)
+        return pltpu.make_async_copy(pair_ref.at[span], pair_hbm.at[span], pair_sem.at[n])
+
+    for step in range(STEPS):
+        pair_part(step)
+        if step == STEPS // 2 - 1:
+            pair_copy(0).start()
+    pair_copy(1).start()
     values = al_ref[...].astype(F32)
     center = values - jnp.mean(values, -1, keepdims=True)
     inverse = lax.rsqrt(jnp.mean(center * center, -1, keepdims=True) + 1e-05)
     normal = center * inverse
     w2 = (am_ref[...] * rm_ref[...]).astype(F32)
+    right_at, left_at = [], []
+    row, lane = iota((128, WIDTH), 0), iota((128, WIDTH), 1)
+    for s in range(2):
+        right_at.append(mm(onehot(row == lane + s * WIDTH), wr_ref[...]).astype(BF16))
+        for h in range(2):
+            left_at.append(mm(onehot(row == lane + (2 * h + s) * WIDTH), wl_ref[...]).astype(BF16))
+    columns = [as_column(w2[s : s + 1]) for s in range(2)]
+    for group in (z_r, z_l, xy_r, x_l, c_r, c_w, c_g, xy_w, z_w, xy_g, x_g):
+        group.sent()
+    xy_f.wait()
+    c_f = core_group(3, lambda o: fin.at[core], lambda n: fin.at[n])
+    c_f.start()
     zl_g.wait()
     left = split(total(lz, 0, 4))
     z_g.wait()
@@ -419,23 +432,15 @@
     order = onehot(col == ((r // 4) % 4) * 16 + (r // 16) * 4 + r % 4)
     right = split(jnp.concatenate([total(rzin, n * 4, 4) for n in range(4)], axis=0))
     right = [mm(order, v).astype(BF16) for v in right]
-    row, lane = iota((128, WIDTH), 0), iota((128, WIDTH), 1)
     for s in range(2):
-        right_at = mm(onehot(row == lane + s * WIDTH), wr_ref[...]).astype(BF16)
-        parts = []
-        for h in range(2):
-            left_at = mm(onehot(row == lane + (2 * h + s) * WIDTH), wl_ref[...]).astype(BF16)
-            parts.append(mm(left[0], left_at) + mm(left[1], left_at))
-        grad = jnp.concatenate(parts, axis=0) + mm(right[0], right_at) + mm(right[1], right_at)
-        grad = grad * as_column(w2[s : s + 1])
+        parts = [sum(mm(v, left_at[2 * s + h]) for v in left) for h in range(2)]
+        grad = jnp.concatenate(parts, axis=0) + sum(mm(v, right_at[s]) for v in right)
+        grad = grad * columns[s]
         span = slice(s * RES, (s + 1) * RES)
         first = jnp.mean(grad, -1, keepdims=True)
         second = jnp.mean(grad * normal[span], -1, keepdims=True)
         ag_ref[span] = (inverse[span] * (grad - first - normal[span] * second)).astype(BF16)
-    xy_f.wait()
-    c_f = core_group(3, lambda o: fin.at[core], lambda n: fin.at[n])
-    c_f.start()
-    for group in (z_r, z_l, xy_r, x_l, c_r, c_w, c_g, xy_w, z_w, xy_f, xy_g, z_g, x_g, zl_g, c_f):
+    for group in (xy_f, z_g, zl_g, c_f):
         group.sent()
     for n in range(2):
         pair_copy(n).wait()

time: 88 us -> 84.1 us (0.956); the launches traced: 87.8 us -> 82.8 us
  Pallas kernels: 87 us -> 82 us
    pallas_call x1, Pallas kernels: 83.9 us -> 78.9 us  [shards(): pl.pallas_call(kernel, out_shape=(jax.ShapeDtypeStruct((RES, COLS, PAIR),...]
where the time goes in v6:
time: 84.1 us; the launch traced here: 82.8 us
  Pallas kernels  82 us (98%)
    pallas_call x1, Pallas kernels, shards(): pl.pallas_call(kernel, out_shape=(jax.ShapeDtypeStruct((RES, COLS, PAIR),...  78.9 us
    pallas_call x1, Pallas kernels, shards(): pl.pallas_call(write_kernel, out_shape=(jax.ShapeDtypeStruct((RES, COLS,...  3.11 us

profile of v6, /device:TPU:1, one launch (start us, length us, event | category | flops | bytes accessed | tf_op | source)
XLA Modules:
  0.0 82.8 jit_solution(10336194929402480668)
XLA Ops:
  0.6 78.9 %pair_update.1 = (bf16[64,128,128]{2,1,0:T(8,128)(2,1)}, bf16[128,256]{1,0:T(8,128)(2,1)}, bf16[2,16,32,128]{3,2,1,0:T(8,128)(2,1)}) custom-call(bf16[128,256]{1,0:T(8,128)(2,1)} %bitcast.8, s32[2,64]{1,0:T(2,128)} %am_hbm.1, s32[1,64]{1,0:T(1,128)} %bitcast.11, bf16[32,256]{1,0:T(8,128)(2,1)} %bitcast.9, bf16[32,256]{1,0:T(8,128)(2,1)} %bitcast.10, ...), custom_call_target="tpu_custom_call" | custom-call | tf_op jit(solution)/shard_map/pair_update/pallas_call | solution.py:481
  79.5 3.1 %write_outputs.1 = (bf16[64,128,128]{2,1,0:T(8,128)(2,1)}, bf16[128,256]{1,0:T(8,128)(2,1)}, f32[1024,128]{1,0:T(8,128)}) custom-call(bf16[64,128,128]{2,1,0:T(8,128)(2,1)} %get-tuple-element.9.pair_in, bf16[128,256]{1,0:T(8,128)(2,1)} %get-tuple-element.10.ag_in, bf16[2,16,32,128]{3,2,1,0:T(8,128)(2,1)} %get-tuple-element.11.fin_in), custom_call_target="tpu_custom_call" | custom-call | tf_op jit(solution)/shard_map/write_outputs/pallas_call | solution.py:525

commit v7 on v6

--- a/solution.py
+++ b/solution.py
@@ -94,10 +94,10 @@
 
 def kernel(
     al_hbm, am_hbm, rm_hbm, wl_hbm, wr_hbm, w_hbm, ct_hbm,
-    pair_hbm, ag_ref, fin,
+    pair_hbm, ag_hbm, fin_hbm,
     al_ref, am_ref, rm_ref, wl_ref, wr_ref, w_ref, ct_ref, in_sem,
     mask_ref, rsend, ra, rb, xr, lall,
-    wf, wn, w4, lf, l2, lt, perm, rp, rm_all, rds, rt, rden, n_all, t_all, sc, rg, lgs, dw, pair_ref, pair_sem,
+    wf, wn, w4, lf, l2, lt, perm, rp, rm_all, rds, rt, rden, n_all, t_all, sc, rg, lgs, dw, pair_ref, ag_ref, fin, out_sem,
     wmsg, wcin, whalf, wxin, wz,
     rmsg, rcin, rhalf, rxin, rzs, rzin,
     lmsg, lx, lhalf, lz,
@@ -273,7 +273,7 @@
     right_mask = mm(order, rm_all[...].astype(BF16)).astype(BF16)
     rden[...] = 1.0 / jnp.maximum(mm(right_mask, left_mask), 1.0)
     right = mm(order, rp[...]).astype(BF16)
-    rds[...] = mm(right, perm[...]).astype(BF16)
+    rp[...] = right
     rt[...] = mm_nt(perm[...], right).astype(BF16)
 
     def scale_of(step):
@@ -389,6 +389,8 @@
     zl_g.start()
     lz[zh] = lhalf[zh]
 
+    rds[...] = mm(rp[...], perm[...]).astype(BF16)
+
     def pair_part(step):
         scale = scale_of(step)
         for k2 in range(BLOCK // 2):
@@ -401,7 +403,7 @@
 
     def pair_copy(n):
         span = pl.ds(n * (RES // 2), RES // 2)
-        return pltpu.make_async_copy(pair_ref.at[span], pair_hbm.at[span], pair_sem.at[n])
+        return pltpu.make_async_copy(pair_ref.at[span], pair_hbm.at[span], out_sem.at[n])
 
     for step in range(STEPS):
         pair_part(step)
@@ -423,8 +425,10 @@
     for group in (z_r, z_l, xy_r, x_l, c_r, c_w, c_g, xy_w, z_w, xy_g, x_g):
         group.sent()
     xy_f.wait()
-    c_f = core_group(3, lambda o: fin.at[core], lambda n: fin.at[n])
+    c_f = core_group(3, lambda o: fin.at[core], lambda n: fin_hbm.at[n])
     c_f.start()
+    fin_copy = pltpu.make_async_copy(fin.at[core], fin_hbm.at[core], out_sem.at[2])
+    fin_copy.start()
     zl_g.wait()
     left = split(total(lz, 0, 4))
     z_g.wait()
@@ -440,8 +444,12 @@
         first = jnp.mean(grad, -1, keepdims=True)
         second = jnp.mean(grad * normal[span], -1, keepdims=True)
         ag_ref[span] = (inverse[span] * (grad - first - normal[span] * second)).astype(BF16)
+    ag_copy = pltpu.make_async_copy(ag_ref, ag_hbm, out_sem.at[3])
+    ag_copy.start()
     for group in (xy_f, z_g, zl_g, c_f):
         group.sent()
+    fin_copy.wait()
+    ag_copy.wait()
     for n in range(2):
         pair_copy(n).wait()
     c_f.wait()
@@ -486,7 +494,7 @@
             jax.ShapeDtypeStruct((2, 16, WIDTH, PAIR), BF16),
         ),
         in_specs=[pl.BlockSpec(memory_space=pltpu.HBM)] * 7,
-        out_specs=(pl.BlockSpec(memory_space=pl.ANY),) + (pl.BlockSpec(memory_space=pltpu.VMEM),) * 2,
+        out_specs=(pl.BlockSpec(memory_space=pl.ANY),) * 3,
         scratch_shapes=[
             vmem((2 * RES, CH), BF16), vmem((2, RES), jnp.int32), vmem((1, RES), jnp.int32),
             vmem((WIDTH, CH), BF16), vmem((WIDTH, CH), BF16), vmem((SIZE, PAIR), BF16),
@@ -501,7 +509,7 @@
             vmem((STEPS, SIZE, BLOCK * PAIR), BF16), vmem((STEPS, BLOCK * SEQS, WIDTH * PAIR), BF16),
             vmem((STEPS, COLS, BLOCK * PAIR), BF16), vmem((SIZE, COLS), F32),
             vmem((RES * SEQS, 128), F32), vmem((WIDTH, WIDTH * PAIR), F32),
-            vmem((RES, COLS, PAIR), BF16), dma((2,)),
+            vmem((RES, COLS, PAIR), BF16), vmem((2 * RES, CH), BF16), vmem((2, 16, WIDTH, PAIR), BF16), dma((4,)),
             vmem((2, 16, 32, 128), BF16), vmem((16, 32, 128), BF16), vmem((16, 32, 128), BF16),
             vmem((16, 32, 128), BF16), vmem((16, 32, 128), BF16),
             vmem((2, 16, 32, 128), BF16), vmem((16, 32, 128), BF16), vmem((16, 32, 128), BF16),

time: 84.1 us -> 83.4 us (level)
  no operation moved by 1% of the time
where the time goes in v7:
time: 83.4 us; the launch traced here: 82.2 us
  Pallas kernels  81.4 us (98%)
  between operations  0.84 us (1%)
    pallas_call x1, Pallas kernels, shards(): pl.pallas_call(kernel, out_shape=(jax.ShapeDtypeStruct((RES, COLS, PAIR),...  78.3 us
    pallas_call x1, Pallas kernels, shards(): pl.pallas_call(write_kernel, out_shape=(jax.ShapeDtypeStruct((RES, COLS,...  3.11 us

profile of v7, /device:TPU:1, one launch (start us, length us, event | category | flops | bytes accessed | tf_op | source)
XLA Modules:
  0.0 82.2 jit_solution(16397976238385383145)
XLA Ops:
  0.6 78.3 %pair_update.1 = (bf16[64,128,128]{2,1,0:T(8,128)(2,1)}, bf16[128,256]{1,0:T(8,128)(2,1)}, bf16[2,16,32,128]{3,2,1,0:T(8,128)(2,1)}) custom-call(bf16[128,256]{1,0:T(8,128)(2,1)} %bitcast.8, s32[2,64]{1,0:T(2,128)} %am_hbm.1, s32[1,64]{1,0:T(1,128)} %bitcast.11, bf16[32,256]{1,0:T(8,128)(2,1)} %bitcast.9, bf16[32,256]{1,0:T(8,128)(2,1)} %bitcast.10, ...), custom_call_target="tpu_custom_call" | custom-call | tf_op jit(solution)/shard_map/pair_update/pallas_call | solution.py:489
  78.9 3.1 %write_outputs.1 = (bf16[64,128,128]{2,1,0:T(8,128)(2,1)}, bf16[128,256]{1,0:T(8,128)(2,1)}, f32[1024,128]{1,0:T(8,128)}) custom-call(bf16[64,128,128]{2,1,0:T(8,128)(2,1)} %get-tuple-element.9.pair_in, bf16[128,256]{1,0:T(8,128)(2,1)} %get-tuple-element.10.ag_in, bf16[2,16,32,128]{3,2,1,0:T(8,128)(2,1)} %get-tuple-element.11.fin_in), custom_call_target="tpu_custom_call" | custom-call | tf_op jit(solution)/shard_map/write_outputs/pallas_call | solution.py:533
